TPU v7x, 512 devices: a whole 4x8x8 slice. The times are simulated.
512 devices in a mesh: seq: 64 (over x, y, core), head: 8 (over z).
Axes of the slice: x: 4, y: 8, z: 8, core: 2. Of those that a mesh axis runs over, the one named last changes fastest.
Arguments:
- query_rows: bfloat16 [32768, 1024], P(('seq', 'head')), may hold values from -16 to 16
- key_rows: bfloat16 [32768, 1024], P(('seq', 'head')), may hold values from -16 to 16
- value_rows: bfloat16 [32768, 1024], P(('seq', 'head')), may hold values from -6 to 6
- out_grad: bfloat16 [32768, 1024], P(('seq', 'head')), may hold values from -6 to 6
- random_blocks: int32 [512, 2], P('seq'), may hold values from 0 to 511, as said below
- global_blocks: int32 [2], replicated, may hold values from 0 to 511
Outputs:
- attn_out: bfloat16 [32768, 1024], P(('seq', 'head'))
- q_grad: bfloat16 [32768, 1024], P(('seq', 'head'))
- k_grad: bfloat16 [32768, 1024], P(('seq', 'head'))
- v_grad: bfloat16 [32768, 1024], P(('seq', 'head'))
Inputs may be any that keep to these rules, and one draw needn't show every extreme that they name: `random_blocks`: the 16 random blocks named by the query blocks of one device belong to 16 different devices along `seq`: at most one of them lies among any one device's 8 blocks.
All inputs are finite; a program needn't handle non-finite values.
Results may differ from a plain program's by a relative error of at most 0.011.
Values may be sent and summed in bfloat16 or wider, within the bound.
No kernel may reach another device: no remote copies, remote signals or barrier semaphores. Data moves between devices by JAX's collectives and lax.ppermute only.
A program may use at most 64 MiB of HBM per device.

v0:
```python
from functools import partial

import jax
import jax.numpy as jnp
from jax import lax
from jax.sharding import PartitionSpec as P

HEAD_DIM = 64
BLOCK = 64
RANDOM = 2
GLOBALS = 2


masked_score = -1e30


def extended(x, sides, width):
    for axis, dim in sides:
        peers, length = (lax.axis_size(axis), x.shape[dim])
        up = [(i, (i + 1) % peers) for i in range(peers - 1)]
        down = [(j, i) for i, j in up]
        last = lax.slice_in_dim(x, length - width, length, axis=dim)
        initial = lax.slice_in_dim(x, 0, width, axis=dim)
        before = lax.ppermute(last, axis, up)
        after = lax.ppermute(initial, axis, down)
        x = jnp.concatenate([before, x, after], axis=dim)
    return x


def broadcast(value, axis, source):
    kept = jnp.where(lax.axis_index(axis) == source, value, 0).astype(value.dtype)
    return lax.psum(kept, axis)


def shifted(value, axis, steps):
    count = lax.axis_size(axis)
    initial, last = (max(0, -steps), min(count, count - steps))
    return lax.ppermute(value, axis, [(source, source + steps) for source in range(initial, last)])


def slot_table(flat_ids, per_device, capacity):
    source = flat_ids // per_device
    within = flat_ids % per_device
    order = jnp.arange(flat_ids.shape[0], dtype=jnp.int32)
    earlier = (source[:, None] == source[None, :]) & (order[None, :] < order[:, None])
    rank = jnp.sum(earlier.astype(jnp.int32), axis=1)
    return (source * capacity + rank, within)


def attend_group(packed, scale_factor, width_here):
    query_group, pair_all, grad_group, key_ok = packed
    groups, block_rows = (query_group.shape[0], query_group.shape[1])
    key_count = pair_all.shape[1]
    head_count = width_here // HEAD_DIM
    query_heads = query_group.reshape(groups, block_rows, head_count, HEAD_DIM)
    grad_heads = grad_group.reshape(groups, block_rows, head_count, HEAD_DIM)
    key_heads = pair_all[:, :, :width_here].reshape(groups, key_count, head_count, HEAD_DIM)
    value_heads = pair_all[:, :, width_here:].reshape(groups, key_count, head_count, HEAD_DIM)
    scores = (
        jnp.einsum("gqhd,gkhd->ghqk", query_heads, key_heads, preferred_element_type=jnp.float32)
        * scale_factor
    )
    scores = jnp.where(key_ok[:, None, None, :], scores, masked_score)
    row_max = jnp.max(scores, axis=-1, keepdims=True)
    weights_raw = jnp.exp(scores - row_max)
    probabilities = weights_raw / jnp.sum(weights_raw, axis=-1, keepdims=True)
    probs_half = probabilities.astype(jnp.bfloat16)
    attended = jnp.einsum(
        "ghqk,gkhd->gqhd", probs_half, value_heads, preferred_element_type=jnp.float32
    )
    prob_grad = jnp.einsum(
        "gqhd,gkhd->ghqk", grad_heads, value_heads, preferred_element_type=jnp.float32
    )
    row_delta = jnp.sum(grad_heads.astype(jnp.float32) * attended, axis=-1).transpose(0, 2, 1)[
        ..., None
    ]
    score_grad = (probabilities * (prob_grad - row_delta)).astype(jnp.bfloat16)
    query_grad = (
        jnp.einsum("ghqk,gkhd->gqhd", score_grad, key_heads, preferred_element_type=jnp.float32)
        * scale_factor
    )
    key_grad = (
        jnp.einsum("ghqk,gqhd->gkhd", score_grad, query_heads, preferred_element_type=jnp.float32)
        * scale_factor
    )
    value_grad = jnp.einsum(
        "ghqk,gqhd->gkhd", probs_half, grad_heads, preferred_element_type=jnp.float32
    )
    pair_grad = jnp.concatenate(
        [
            key_grad.reshape(groups, key_count, width_here),
            value_grad.reshape(groups, key_count, width_here),
        ],
        axis=-1,
    )
    pair_grad = pair_grad.reshape(groups, key_count // block_rows, block_rows, 2 * width_here)
    window_part = pair_grad[:, 0:3]
    random_part = pair_grad[:, 3 : 3 + RANDOM].astype(jnp.bfloat16)
    global_part = jnp.sum(pair_grad[:, 3 + RANDOM :], axis=0)
    attended_half = attended.reshape(groups, block_rows, width_here).astype(jnp.bfloat16)
    query_half = query_grad.reshape(groups, block_rows, width_here).astype(jnp.bfloat16)
    return (attended_half, query_half, window_part, random_part, global_part)


def body(query_rows, key_rows, value_rows, out_grad, random_blocks, global_blocks):
    query_here, key_here, value_here, grad_here = (
        lax.all_to_all(query_rows, "head", split_axis=1, concat_axis=0, tiled=True),
        lax.all_to_all(key_rows, "head", split_axis=1, concat_axis=0, tiled=True),
        lax.all_to_all(value_rows, "head", split_axis=1, concat_axis=0, tiled=True),
        lax.all_to_all(out_grad, "head", split_axis=1, concat_axis=0, tiled=True),
    )
    tokens_here, width_here = query_here.shape
    blocks_here = tokens_here // BLOCK
    seq_devices = lax.axis_size("seq")
    my_index = lax.axis_index("seq")
    capacity = max(1, RANDOM * blocks_here // seq_devices)
    slot_total = seq_devices * capacity
    request_total = RANDOM * blocks_here
    scale_factor = HEAD_DIM ** (-0.5)
    pair_rows = jnp.concatenate([key_here, value_here], axis=1)
    pair_blocks = pair_rows.reshape(blocks_here, BLOCK, 2 * width_here)
    padded = extended(pair_rows, (("seq", 0),), BLOCK)
    padded_blocks = padded.reshape(blocks_here + 2, BLOCK, 2 * width_here)
    window_rows = jnp.stack(
        [
            padded_blocks[0:blocks_here],
            padded_blocks[1 : blocks_here + 1],
            padded_blocks[2 : blocks_here + 2],
        ],
        axis=1,
    )
    flat_ids = random_blocks.reshape(request_total)
    slot_of, within_of = slot_table(flat_ids, blocks_here, capacity)
    slot_iota = jnp.arange(slot_total, dtype=jnp.int32)
    slot_hit = slot_of[:, None] == slot_iota[None, :]
    asked_for = jnp.sum(jnp.where(slot_hit, within_of[:, None], 0), axis=0).reshape(
        seq_devices, capacity
    )
    served = lax.all_to_all(asked_for, "seq", split_axis=0, concat_axis=0, tiled=True)
    served_flat = served.reshape(slot_total)
    outgoing = jnp.take(pair_blocks, served_flat, axis=0).reshape(
        seq_devices, capacity, BLOCK, 2 * width_here
    )
    incoming = lax.all_to_all(outgoing, "seq", split_axis=0, concat_axis=0, tiled=True).reshape(
        slot_total, BLOCK, 2 * width_here
    )
    picked = jnp.take(incoming, slot_of, axis=0).reshape(blocks_here, RANDOM, BLOCK, 2 * width_here)
    owners = global_blocks // blocks_here
    owned_at = global_blocks % blocks_here
    fetched = []
    for global_slot in range(GLOBALS):
        piece = lax.dynamic_index_in_dim(pair_blocks, owned_at[global_slot], 0, keepdims=False)
        fetched.append(broadcast(piece, "seq", owners[global_slot]))
    global_pair = jnp.stack(fetched, axis=0)
    global_every = jnp.broadcast_to(
        global_pair[None], (blocks_here, GLOBALS, BLOCK, 2 * width_here)
    )
    pair_all = jnp.concatenate([window_rows, picked, global_every], axis=1).reshape(
        blocks_here, -1, 2 * width_here
    )
    block_number = my_index * blocks_here + jnp.arange(blocks_here, dtype=jnp.int32)
    total_blocks = blocks_here * seq_devices
    part_ok = jnp.ones((blocks_here, 3 + RANDOM + GLOBALS), jnp.bool_)
    part_ok = part_ok.at[:, 0].set(block_number > 0).at[:, 2].set(block_number < total_blocks - 1)
    key_ok = jnp.repeat(part_ok, BLOCK, axis=1)
    group_size = min(blocks_here, max(1, 512 // BLOCK))
    group_count = blocks_here // group_size

    def regroup(tensor):
        return tensor.reshape((group_count, group_size) + tensor.shape[1:])

    packed = (
        regroup(query_here.reshape(blocks_here, BLOCK, width_here)),
        regroup(pair_all),
        regroup(grad_here.reshape(blocks_here, BLOCK, width_here)),
        regroup(key_ok),
    )
    attended, query_grad, window_grad, random_grad, global_grad = lax.map(
        partial(attend_group, scale_factor=scale_factor, width_here=width_here), packed
    )
    attended = attended.reshape(tokens_here, width_here)
    query_grad = query_grad.reshape(tokens_here, width_here)
    window_grad = window_grad.reshape(blocks_here, 3, BLOCK, 2 * width_here)
    window_sum = (
        jnp.pad(window_grad[:, 0], ((0, 2), (0, 0), (0, 0)))
        + jnp.pad(window_grad[:, 1], ((1, 1), (0, 0), (0, 0)))
        + jnp.pad(window_grad[:, 2], ((2, 0), (0, 0), (0, 0)))
    )
    from_above = shifted(window_sum[0].astype(jnp.bfloat16), "seq", -1).astype(jnp.float32)
    from_below = shifted(window_sum[blocks_here + 1].astype(jnp.bfloat16), "seq", 1).astype(
        jnp.float32
    )
    owned_grad = window_sum[1 : blocks_here + 1]
    owned_grad = owned_grad.at[blocks_here - 1].add(from_above).at[0].add(from_below)
    random_flat = random_grad.reshape(request_total, BLOCK, 2 * width_here)
    slot_used = jnp.any(slot_hit, axis=0)
    source_request = jnp.sum(
        jnp.where(slot_hit, jnp.arange(request_total, dtype=jnp.int32)[:, None], 0), axis=0
    )
    sending = jnp.where(
        slot_used[:, None, None],
        jnp.take(random_flat, source_request, axis=0),
        jnp.zeros((), jnp.bfloat16),
    )
    sending = sending.reshape(seq_devices, capacity, BLOCK, 2 * width_here)
    returned = lax.all_to_all(sending, "seq", split_axis=0, concat_axis=0, tiled=True).reshape(
        slot_total, BLOCK * 2 * width_here
    )
    owner_hit = (served_flat[None, :] == jnp.arange(blocks_here, dtype=jnp.int32)[:, None]).astype(
        jnp.bfloat16
    )
    owned_grad = owned_grad + jnp.dot(
        owner_hit, returned, preferred_element_type=jnp.float32
    ).reshape(blocks_here, BLOCK, 2 * width_here)
    global_total = lax.psum(jnp.sum(global_grad, axis=0), "seq")
    block_iota = jnp.arange(blocks_here, dtype=jnp.int32)
    for global_slot in range(GLOBALS):
        hit_mask = (block_iota == owned_at[global_slot]) & (owners[global_slot] == my_index)
        owned_grad = owned_grad + jnp.where(
            hit_mask[:, None, None], global_total[global_slot][None], 0.0
        )
    pair_grad = owned_grad.reshape(tokens_here, 2 * width_here).astype(jnp.bfloat16)
    return (
        lax.all_to_all(attended, "head", split_axis=0, concat_axis=1, tiled=True),
        lax.all_to_all(query_grad, "head", split_axis=0, concat_axis=1, tiled=True),
        lax.all_to_all(pair_grad[:, :width_here], "head", split_axis=0, concat_axis=1, tiled=True),
        lax.all_to_all(pair_grad[:, width_here:], "head", split_axis=0, concat_axis=1, tiled=True),
    )


def solution(mesh):
    placed = (
        P(("seq", "head"), None),
        P(("seq", "head"), None),
        P(("seq", "head"), None),
        P(("seq", "head"), None),
        P("seq", None),
        P(),
    )
    return jax.shard_map(
        body,
        mesh=mesh,
        in_specs=placed,
        out_specs=(
            P(("seq", "head"), None),
            P(("seq", "head"), None),
            P(("seq", "head"), None),
            P(("seq", "head"), None),
        ),
        check_vma=False,
    )
```

profile of v0, /device:TPU:1, one launch (start us, length us, event | category | flops | bytes accessed | tf_op | source)
XLA Modules:
  0.0 582.2 jit_solution(378194306207217572)
XLA Ops:
  9.1 11.6 %all-to-all-start.2 = ((s32[64,1,1]{2,1,0:T(1,128)}), s32[64,1,1]{2,1,0:T(1,128)S(1)}, u32[]{:S(2)}, u32[]{:S(2)}) async-start(s32[64,1,1]{2,1,0:T(1,128)} %copy.164), calls=%async_computation.2 | async-start | bytes 65536 | tf_op jit(solution)/shard_map/all_to_all | solution.py:139
  24.5 5.4 all-to-all-done.2
  29.9 10.0 %all-to-all-start = ((bf16[64,8,128]{2,0,1:T(8,128)(2,1)}), bf16[64,8,128]{2,0,1:T(8,128)(2,1)S(1)}, u32[]{:S(2)}, u32[]{:S(2)}) async-start(bf16[64,8,128]{2,0,1:T(8,128)(2,1)} %copy_bitcast_fusion.7), calls=%async_computation | async-start | bytes 262144 | tf_op jit(solution)/shard_map/all_to_all | solution.py:108
  42.7 5.0 all-to-all-done
  47.7 3.4 all-to-all-start.1
  51.1 7.9 %all-to-all-done.1 = bf16[64,8,128]{2,0,1:T(8,128)(2,1)S(1)} async-done(((bf16[64,8,128]{2,0,1:T(8,128)(2,1)}), bf16[64,8,128]{2,0,1:T(8,128)(2,1)S(1)}, u32[]{:S(2)}, u32[]{:S(2)}) %all-to-all-start.1) | async-done | bytes 131104 | tf_op jit(solution)/shard_map/all_to_all | solution.py:109
  59.0 3.4 all-to-all-start.4
  63.2 7.2 %all-to-all-done.4 = bf16[64,8,128]{2,0,1:T(8,128)(2,1)S(1)} async-done(((bf16[64,8,128]{2,0,1:T(8,128)(2,1)}), bf16[64,8,128]{2,0,1:T(8,128)(2,1)S(1)}, u32[]{:S(2)}, u32[]{:S(2)}) %all-to-all-start.4) | async-done | bytes 131104 | tf_op jit(solution)/shard_map/all_to_all | solution.py:107
  70.4 3.4 all-to-all-start.6
  75.3 6.2 %all-to-all-done.6 = bf16[64,8,128]{2,0,1:T(8,128)(2,1)S(1)} async-done(((bf16[64,8,128]{2,0,1:T(8,128)(2,1)}), bf16[64,8,128]{2,0,1:T(8,128)(2,1)S(1)}, u32[]{:S(2)}, u32[]{:S(2)}) %all-to-all-start.6) | async-done | bytes 131104 | tf_op jit(solution)/shard_map/all_to_all | solution.py:110
  81.6 10.1 %all-to-all-start.3 = ((bf16[64,1,64,256]{3,2,1,0:T(8,128)(2,1)}), bf16[64,1,64,256]{3,2,1,0:T(8,128)(2,1)S(1)}, u32[]{:S(2)}, u32[]{:S(2)}) async-start(bf16[64,1,64,256]{3,2,1,0:T(8,128)(2,1)} %fusion.9), calls=%async_computation.3 | async-start | bytes 4194304 | tf_op jit(solution)/shard_map/all_to_all | solution.py:144
  108.2 172.2 %all-reduce.10.cloned.1.call-done = (bf16[1,64,256]{2,1,0:T(8,128)(2,1)}, bf16[1,64,256]{2,1,0:T(8,128)(2,1)}) async-done(((bf16[1,64,256]{2,1,0:T(8,128)(2,1)}, bf16[1,64,256]{2,1,0:T(8,128)(2,1)}), (bf16[1,64,256]{2,1,0:T(8,128)(2,1)}, bf16[1,64,256]{2,1,0:T(8,128)(2,1)})) %all-reduce.10.cloned.1.call-update) | async-done | bytes 65552 | tf_op jit(solution)/shard_map/psum | solution.py:32
  296.2 7.1 %all-to-all-start.5 = ((bf16[8,64,128]{2,1,0:T(8,128)(2,1)}), bf16[8,64,128]{2,1,0:T(8,128)(2,1)}, u32[]{:S(2)}, u32[]{:S(2)}) async-start(bf16[8,64,128]{2,1,0:T(8,128)(2,1)} %copy.174), calls=%async_computation.5 | async-start | bytes 262144 | tf_op jit(solution)/shard_map/all_to_all | solution.py:224
  308.9 4.5 reshape.553
  313.3 3.7 copy.185
  323.4 6.8 %all-to-all-start.8 = ((bf16[64,1,64,256]{3,2,1,0:T(8,128)(2,1)}), bf16[64,1,64,256]{3,2,1,0:T(8,128)(2,1)}, u32[]{:S(2)}, u32[]{:S(2)}) async-start(bf16[64,1,64,256]{3,2,1,0:T(8,128)(2,1)} %fusion.5), calls=%async_computation.8 | async-start | bytes 4194304 | tf_op jit(solution)/shard_map/all_to_all | solution.py:206
  346.0 32.1 %collective-permute-done.2 = bf16[64,256]{1,0:T(8,128)(2,1)} collective-permute-done((bf16[64,256]{1,0:T(8,128)(2,1)}, bf16[64,256]{1,0:T(8,128)(2,1)}, u32[]{:S(2)}, u32[]{:S(2)}) %collective-permute-start.2) | collective-permute-done | bytes 32800 | tf_op jit(solution)/shard_map/ppermute | solution.py:38
  380.2 152.6 %all-reduce.8.cloned.1.call-done = f32[2,64,256]{2,1,0:T(8,128)} async-done(((f32[2,64,256]{2,1,0:T(8,128)}), f32[2,64,256]{2,1,0:T(8,128)}) %all-reduce.8.cloned.1.call-update) | async-done | bytes 131088 | tf_op jit(solution)/shard_map/psum | solution.py:215
  535.2 7.1 %all-to-all-start.7 = ((bf16[8,64,128]{2,1,0:T(8,128)(2,1)}), bf16[8,64,128]{2,1,0:T(8,128)(2,1)S(1)}, u32[]{:S(2)}, u32[]{:S(2)}) async-start(bf16[8,64,128]{2,1,0:T(8,128)(2,1)} %copy.179), calls=%async_computation.7 | async-start | bytes 262144 | tf_op jit(solution)/shard_map/all_to_all | solution.py:225
  546.0 5.9 %all-to-all-done.7 = bf16[8,64,128]{2,1,0:T(8,128)(2,1)S(1)} async-done(((bf16[8,64,128]{2,1,0:T(8,128)(2,1)}), bf16[8,64,128]{2,1,0:T(8,128)(2,1)S(1)}, u32[]{:S(2)}, u32[]{:S(2)}) %all-to-all-start.7) | async-done | bytes 131104 | tf_op jit(solution)/shard_map/all_to_all | solution.py:225
  551.9 3.4 all-to-all-start.9
  555.9 7.6 %all-to-all-done.9 = bf16[8,64,128]{2,1,0:T(8,128)(2,1)S(1)} async-done(((bf16[8,64,128]{2,1,0:T(8,128)(2,1)}), bf16[8,64,128]{2,1,0:T(8,128)(2,1)S(1)}, u32[]{:S(2)}, u32[]{:S(2)}) %all-to-all-start.9) | async-done | bytes 131104 | tf_op jit(solution)/shard_map/all_to_all | solution.py:226
  563.5 3.4 all-to-all-start.10
  567.6 7.2 %all-to-all-done.10 = bf16[8,64,128]{2,1,0:T(8,128)(2,1)S(1)} async-done(((bf16[8,64,128]{2,1,0:T(8,128)(2,1)}), bf16[8,64,128]{2,1,0:T(8,128)(2,1)S(1)}, u32[]{:S(2)}, u32[]{:S(2)}) %all-to-all-start.10) | async-done | bytes 131104 | tf_op jit(solution)/shard_map/all_to_all | solution.py:227
  (124 shorter events, 74.2 us)
Async XLA Ops:
  7.2 13.5 %copy-start = (bf16[64,1024]{1,0:T(8,128)(2,1)S(1)}, bf16[64,1024]{1,0:T(8,128)(2,1)}, u32[]{:S(2)}) copy-start(bf16[64,1024]{1,0:T(8,128)(2,1)} %param.14) | copy-start | bytes 393220
  9.1 20.8 %all-to-all-start.2 = ((s32[64,1,1]{2,1,0:T(1,128)}), s32[64,1,1]{2,1,0:T(1,128)S(1)}, u32[]{:S(2)}, u32[]{:S(2)}) async-start(s32[64,1,1]{2,1,0:T(1,128)} %copy.164), calls=%async_computation.2 | async-start | bytes 65536 | tf_op jit(solution)/shard_map/all_to_all | solution.py:139
  29.9 17.8 %all-to-all-start = ((bf16[64,8,128]{2,0,1:T(8,128)(2,1)}), bf16[64,8,128]{2,0,1:T(8,128)(2,1)S(1)}, u32[]{:S(2)}, u32[]{:S(2)}) async-start(bf16[64,8,128]{2,0,1:T(8,128)(2,1)} %copy_bitcast_fusion.7), calls=%async_computation | async-start | bytes 262144 | tf_op jit(solution)/shard_map/all_to_all | solution.py:108
  47.7 11.3 %all-to-all-start.1 = ((bf16[64,8,128]{2,0,1:T(8,128)(2,1)}), bf16[64,8,128]{2,0,1:T(8,128)(2,1)S(1)}, u32[]{:S(2)}, u32[]{:S(2)}) async-start(bf16[64,8,128]{2,0,1:T(8,128)(2,1)} %copy_bitcast_fusion.6), calls=%async_computation.1 | async-start | bytes 262144 | tf_op jit(solution)/shard_map/all_to_all | solution.py:109
  59.0 11.3 %all-to-all-start.4 = ((bf16[64,8,128]{2,0,1:T(8,128)(2,1)}), bf16[64,8,128]{2,0,1:T(8,128)(2,1)S(1)}, u32[]{:S(2)}, u32[]{:S(2)}) async-start(bf16[64,8,128]{2,0,1:T(8,128)(2,1)} %copy_bitcast_fusion.5), calls=%async_computation.4 | async-start | bytes 262144 | tf_op jit(solution)/shard_map/all_to_all | solution.py:107
  70.4 11.2 %all-to-all-start.6 = ((bf16[64,8,128]{2,0,1:T(8,128)(2,1)}), bf16[64,8,128]{2,0,1:T(8,128)(2,1)S(1)}, u32[]{:S(2)}, u32[]{:S(2)}) async-start(bf16[64,8,128]{2,0,1:T(8,128)(2,1)} %copy_bitcast_fusion.4), calls=%async_computation.6 | async-start | bytes 262144 | tf_op jit(solution)/shard_map/all_to_all | solution.py:110
  75.3 16.4 %copy-start.10 = (s32[2]{0:T(128)S(1)}, s32[2]{0:T(128)}, u32[]{:S(2)}) copy-start(s32[2]{0:T(128)} %param.19) | copy-start | bytes 28
  81.6 201.9 %all-to-all-start.3 = ((bf16[64,1,64,256]{3,2,1,0:T(8,128)(2,1)}), bf16[64,1,64,256]{3,2,1,0:T(8,128)(2,1)S(1)}, u32[]{:S(2)}, u32[]{:S(2)}) async-start(bf16[64,1,64,256]{3,2,1,0:T(8,128)(2,1)} %fusion.9), calls=%async_computation.3 | async-start | bytes 4194304 | tf_op jit(solution)/shard_map/all_to_all | solution.py:144
  91.7 188.7 %all-reduce.10.cloned.1.call-start = ((), (), s32[]{:S(2)}) async-start(), calls=%async_computation.12 | async-start | bytes 131072 | tf_op jit(solution)/shard_map/psum | solution.py:32
  101.8 186.8 %copy-start.6 = (bf16[8,64,128]{1,2,0:T(8,128)(2,1)}, bf16[8,64,128]{1,2,0:T(8,128)(2,1)S(1)}, u32[]{:S(2)}) copy-start(bf16[8,64,128]{1,2,0:T(8,128)(2,1)S(1)} %copy.199) | copy-start | bytes 393220
  101.8 179.4 %collective-permute-start.1 = (bf16[64,256]{1,0:T(8,128)(2,1)S(1)}, bf16[64,256]{1,0:T(8,128)(2,1)S(1)}, u32[]{:S(2)}, u32[]{:S(2)}) collective-permute-start(bf16[64,256]{1,0:T(8,128)(2,1)S(1)} %get-tuple-element.103), channel_id=1, source_target_pairs={{8,0},{16,8},{24,16},{32,24},{40,32},{48,40},{56,48},{64,56},{72,6... | collective-permute-start | bytes 98312 | tf_op jit(solution)/shard_map/ppermute | solution.py:25
  104.1 177.1 %collective-permute-start = (bf16[64,256]{1,0:T(8,128)(2,1)S(1)}, bf16[64,256]{1,0:T(8,128)(2,1)S(1)}, u32[]{:S(2)}, u32[]{:S(2)}) collective-permute-start(bf16[64,256]{1,0:T(8,128)(2,1)S(1)} %get-tuple-element.104), channel_id=1, source_target_pairs={{0,8},{8,16},{16,24},{24,32},{32,40},{40,48},{48,56},{56,64},{64,7... | collective-permute-start | bytes 98312 | tf_op jit(solution)/shard_map/ppermute | solution.py:24
  288.5 4.4 copy-start.4
  294.8 8.4 %copy-start.7 = (bf16[8,64,128]{1,2,0:T(8,128)(2,1)S(1)}, bf16[8,64,128]{1,2,0:T(8,128)(2,1)}, u32[]{:S(2)}) copy-start(bf16[8,64,128]{1,2,0:T(8,128)(2,1)} %copy-done.6) | copy-start | bytes 393220
  296.2 27.2 %all-to-all-start.5 = ((bf16[8,64,128]{2,1,0:T(8,128)(2,1)}), bf16[8,64,128]{2,1,0:T(8,128)(2,1)}, u32[]{:S(2)}, u32[]{:S(2)}) async-start(bf16[8,64,128]{2,1,0:T(8,128)(2,1)} %copy.174), calls=%async_computation.5 | async-start | bytes 262144 | tf_op jit(solution)/shard_map/all_to_all | solution.py:224
  323.4 211.8 %all-to-all-start.8 = ((bf16[64,1,64,256]{3,2,1,0:T(8,128)(2,1)}), bf16[64,1,64,256]{3,2,1,0:T(8,128)(2,1)}, u32[]{:S(2)}, u32[]{:S(2)}) async-start(bf16[64,1,64,256]{3,2,1,0:T(8,128)(2,1)} %fusion.5), calls=%async_computation.8 | async-start | bytes 4194304 | tf_op jit(solution)/shard_map/all_to_all | solution.py:206
  330.1 202.6 %all-reduce.8.cloned.1.call-start = ((), (), s32[]{:S(2)}) async-start(), calls=%async_computation.11 | async-start | bytes 262144 | tf_op jit(solution)/shard_map/psum | solution.py:215
  334.0 4.1 copy-start.2
  335.7 42.4 %collective-permute-start.2 = (bf16[64,256]{1,0:T(8,128)(2,1)}, bf16[64,256]{1,0:T(8,128)(2,1)}, u32[]{:S(2)}, u32[]{:S(2)}) collective-permute-start(bf16[64,256]{1,0:T(8,128)(2,1)} %get-tuple-element.96), channel_id=1, source_target_pairs={{8,0},{16,8},{24,16},{32,24},{40,32},{48,40},{56,48},{64,56},{72,6... | collective-permute-start | bytes 98312 | tf_op jit(solution)/shard_map/ppermute | solution.py:38
  339.2 6.7 %copy-start.3 = (f32[10,64,256]{2,1,0:T(8,128)S(1)}, f32[10,64,256]{2,1,0:T(8,128)}, u32[]{:S(2)}) copy-start(f32[10,64,256]{2,1,0:T(8,128)} %get-tuple-element.87) | copy-start | bytes 1966084
  342.8 36.0 %collective-permute-start.3 = (bf16[64,256]{1,0:T(8,128)(2,1)S(1)}, bf16[64,256]{1,0:T(8,128)(2,1)S(1)}, u32[]{:S(2)}, u32[]{:S(2)}) collective-permute-start(bf16[64,256]{1,0:T(8,128)(2,1)S(1)} %copy-done.9), channel_id=1, source_target_pairs={{0,8},{8,16},{16,24},{24,32},{32,40},{40,48},{48,56},{56,64},{64,7... | collective-permute-start | bytes 98312 | tf_op jit(solution)/shard_map/ppermute | solution.py:38
  535.2 16.7 %all-to-all-start.7 = ((bf16[8,64,128]{2,1,0:T(8,128)(2,1)}), bf16[8,64,128]{2,1,0:T(8,128)(2,1)S(1)}, u32[]{:S(2)}, u32[]{:S(2)}) async-start(bf16[8,64,128]{2,1,0:T(8,128)(2,1)} %copy.179), calls=%async_computation.7 | async-start | bytes 262144 | tf_op jit(solution)/shard_map/all_to_all | solution.py:225
  551.9 11.6 %all-to-all-start.9 = ((bf16[8,64,128]{2,1,0:T(8,128)(2,1)}), bf16[8,64,128]{2,1,0:T(8,128)(2,1)S(1)}, u32[]{:S(2)}, u32[]{:S(2)}) async-start(bf16[8,64,128]{2,1,0:T(8,128)(2,1)} %bitcast.56), calls=%async_computation.9 | async-start | bytes 262144 | tf_op jit(solution)/shard_map/all_to_all | solution.py:226
  563.5 11.2 %all-to-all-start.10 = ((bf16[8,64,128]{2,1,0:T(8,128)(2,1)}), bf16[8,64,128]{2,1,0:T(8,128)(2,1)S(1)}, u32[]{:S(2)}, u32[]{:S(2)}) async-start(bf16[8,64,128]{2,1,0:T(8,128)(2,1)} %bitcast.58), calls=%async_computation.10 | async-start | bytes 262144 | tf_op jit(solution)/shard_map/all_to_all | solution.py:227
  (5 other events, 12.5 us)
Sparse Core Ops, SparseCore 0:
  101.7 178.6 all-reduce.9
  342.9 189.7 all-reduce.7
where the time goes:
time: 585 us; the launch traced here: 582 us
  waiting for transfers between devices  409 us (70%)
  starting transfers between devices  80.8 us (14%)
  local copies, waits for them, and re-layouts  40.5 us (7%)
  between operations  21.1 us (4%)
  other arithmetic  19.5 us (3%)
  matrix products  11.2 us (2%)
    psum x1, waiting for transfers between devices, broadcast(): return lax.psum(kept, axis)  172 us
    psum x1, waiting for transfers between devices, body(): global_total = lax.psum(jnp.sum(global_grad, axis=0), 'seq')  153 us
    ppermute x2, waiting for transfers between devices, shifted(): lax.ppermute(value, axis, [(source, source + steps) for source in range(i...  32.1 us
    concatenate x4, local copies, waits for them, and re-layouts, attend_group(): jnp.concatenate([key_grad.reshape(groups, key_count, width_here), value_g...  13.3 us
  transfers between devices with their start and end apart: 17, of which 11 were waited for; matrix products, arithmetic and copies ran while one was open for 10% of the time, Pallas kernels for 0%

commit v1 on v0

v1 whole, which is shorter than its diff:
```python
import jax
import jax.numpy as jnp
from jax import lax
from jax.experimental import pallas as pl
from jax.experimental.pallas import tpu as pltpu
from jax.sharding import Mesh
from jax.sharding import PartitionSpec as P

HEAD_DIM = 64
BLOCK = 64
LANES = 128
COLUMN = 16
CHIPS = 32
RANDOMS = 32
UNITS = 40
ROWS = 2
SCALE = HEAD_DIM**-0.5
VMEM = 48 * 1024 * 1024


def vmem_call(kernel, out_shape, scratch=(), **specs):
    return pl.pallas_call(
        kernel,
        out_shape=out_shape,
        scratch_shapes=scratch,
        compiler_params=pltpu.CompilerParams(vmem_limit_bytes=VMEM),
        **specs,
    )


def low_lanes(shape):
    return lax.broadcasted_iota(jnp.int32, shape, len(shape) - 1) < HEAD_DIM


def pack_kernel(q_ref, g_ref, k_ref, v_ref, out_ref):
    low = low_lanes((BLOCK, LANES))
    for row, (a_ref, b_ref) in enumerate(((q_ref, g_ref), (k_ref, v_ref))):
        rows = slice(row * BLOCK, (row + 1) * BLOCK)
        for pair in range(COLUMN // 2):
            lanes = slice(pair * LANES, (pair + 1) * LANES)
            a = a_ref[:, lanes].astype(jnp.float32)
            b = b_ref[:, lanes].astype(jnp.float32)
            a_turned = pltpu.roll(a, HEAD_DIM, 1)
            b_turned = pltpu.roll(b, HEAD_DIM, 1)
            out_ref[2 * pair, rows, :] = jnp.where(low, a, b_turned).astype(jnp.bfloat16)
            out_ref[2 * pair + 1, rows, :] = jnp.where(low, a_turned, b).astype(jnp.bfloat16)


def unpack_kernel(in_ref, o_ref, dq_ref, dk_ref, dv_ref):
    low = low_lanes((BLOCK, LANES))
    for row, (a_ref, b_ref) in enumerate(((dq_ref, o_ref), (dk_ref, dv_ref))):
        rows = slice(row * BLOCK, (row + 1) * BLOCK)
        for pair in range(COLUMN // 2):
            lanes = slice(pair * LANES, (pair + 1) * LANES)
            even = in_ref[2 * pair, rows, :].astype(jnp.float32)
            odd = in_ref[2 * pair + 1, rows, :].astype(jnp.float32)
            even_turned = pltpu.roll(even, HEAD_DIM, 1)
            odd_turned = pltpu.roll(odd, HEAD_DIM, 1)
            a_ref[:, lanes] = jnp.where(low, even, odd_turned).astype(jnp.bfloat16)
            b_ref[:, lanes] = jnp.where(low, even_turned, odd).astype(jnp.bfloat16)


def attend_kernel(edge_ref, own_ref, unit_ref, out_ref, grad_ref, own_grad_ref, edge_grad):
    low = low_lanes((BLOCK, LANES))
    key_low = low_lanes((7 * BLOCK, LANES))
    key_part = lax.broadcasted_iota(jnp.int32, (BLOCK, 7 * BLOCK), 1) // BLOCK
    zero = jnp.zeros((BLOCK, LANES), jnp.bfloat16)
    own_grad_ref[...] = jnp.zeros(own_grad_ref.shape, jnp.float32)
    edge_grad[...] = jnp.zeros(edge_grad.shape, jnp.float32)

    def own_key(block):
        if block < 0:
            return unit_ref[RANDOMS + 2]
        if block >= COLUMN:
            return unit_ref[RANDOMS + 3]
        return own_ref[block, BLOCK:, :]

    for block in range(COLUMN):
        pair = own_ref[block, :BLOCK, :]
        rows = jnp.concatenate([jnp.where(low, pair, zero), jnp.where(low, zero, pair)], axis=0)
        keys = jnp.concatenate(
            [
                own_key(block - 1),
                own_key(block),
                own_key(block + 1),
                unit_ref[2 * block],
                unit_ref[2 * block + 1],
                unit_ref[RANDOMS],
                unit_ref[RANDOMS + 1],
            ],
            axis=0,
        )
        both = lax.dot_general(
            rows, keys, (((1,), (1,)), ((), ())), preferred_element_type=jnp.float32
        )
        scores = both[:BLOCK] * SCALE
        prob_grad = both[BLOCK:]
        if block == 0:
            scores = jnp.where((key_part == 0) & (edge_ref[0] != 0), -1e30, scores)
        if block == COLUMN - 1:
            scores = jnp.where((key_part == 2) & (edge_ref[1] != 0), -1e30, scores)
        raised = jnp.exp(scores - jnp.max(scores, axis=1, keepdims=True))
        probabilities = raised / jnp.sum(raised, axis=1, keepdims=True)
        probs_half = probabilities.astype(jnp.bfloat16)
        row_delta = jnp.sum(probs_half.astype(jnp.float32) * prob_grad, axis=1, keepdims=True)
        score_grad = (probabilities * (prob_grad - row_delta)).astype(jnp.bfloat16)
        stacked = jnp.concatenate([score_grad, probs_half], axis=0)
        mixed = jnp.dot(stacked, keys, preferred_element_type=jnp.float32)
        out_ref[block] = jnp.where(low, mixed[:BLOCK] * SCALE, mixed[BLOCK:]).astype(jnp.bfloat16)
        part = lax.dot_general(
            stacked, rows, (((0,), (0,)), ((), ())), preferred_element_type=jnp.float32
        )
        part = jnp.where(key_low, part * SCALE, part)
        for step in range(3):
            grad = part[step * BLOCK : (step + 1) * BLOCK]
            where = block + step - 1
            if where < 0:
                grad_ref[RANDOMS + 2] = grad.astype(jnp.bfloat16)
            elif where >= COLUMN:
                grad_ref[RANDOMS + 3] = grad.astype(jnp.bfloat16)
            else:
                own_grad_ref[where] += grad
        for step in range(2):
            grad_ref[2 * block + step] = part[(3 + step) * BLOCK : (4 + step) * BLOCK].astype(
                jnp.bfloat16
            )
            edge_grad[step] += part[(5 + step) * BLOCK : (6 + step) * BLOCK]
    for step in range(2):
        grad_ref[RANDOMS + step] = edge_grad[step].astype(jnp.bfloat16)
    for unit in range(RANDOMS + 4, UNITS):
        grad_ref[unit] = zero


def swap(value, axis):
    return lax.all_to_all(value, axis, split_axis=0, concat_axis=0, tiled=True)


def body(query_rows, key_rows, value_rows, out_grad, random_blocks, global_blocks):
    chip, core = lax.axis_index("chip"), lax.axis_index("core")
    half = jnp.bfloat16
    column = ("core", "head")

    packed = vmem_call(pack_kernel, jax.ShapeDtypeStruct((COLUMN, 2 * BLOCK, LANES), half))(
        query_rows, out_grad, key_rows, value_rows
    )
    own = swap(packed, column)

    other = lax.ppermute(random_blocks, "core", [(0, 1), (1, 0)])
    mine = random_blocks.reshape(1, -1)
    other = other.reshape(1, -1)
    named = jnp.where(
        core == 0, jnp.concatenate([mine, other], 1), jnp.concatenate([other, mine], 1)
    )
    named = jnp.concatenate([named // 8, named % 8], 0).astype(half)
    named = jnp.pad(named, ((0, 6), (0, LANES - RANDOMS)))

    spread = own[:, BLOCK:].reshape(COLUMN, ROWS, CHIPS, LANES).transpose(2, 1, 0, 3)
    spread = spread.reshape(CHIPS, ROWS * COLUMN, LANES)
    spread = jnp.concatenate([spread, jnp.broadcast_to(named[None], (CHIPS, 8, LANES))], axis=1)
    held = swap(spread, "chip")

    blocks = CHIPS * COLUMN
    table = jnp.concatenate(
        [held[:, r * COLUMN : (r + 1) * COLUMN].reshape(blocks, LANES) for r in range(ROWS)], axis=1
    )
    ids = held[:, 2 * COLUMN : 2 * COLUMN + 2, :RANDOMS].astype(jnp.float32)
    ids = (ids[:, 0] * 8 + ids[:, 1]).astype(jnp.int32)
    first = jnp.arange(CHIPS, dtype=jnp.int32)[:, None] * COLUMN
    ids = jnp.concatenate(
        [
            ids,
            jnp.broadcast_to(global_blocks[None], (CHIPS, 2)),
            first - 1,
            jnp.where(first + COLUMN < blocks, first + COLUMN, -1),
            jnp.full((CHIPS, UNITS - RANDOMS - 4), -1, jnp.int32),
        ],
        axis=1,
    ).reshape(-1)
    block_iota = jnp.arange(blocks, dtype=jnp.int32)
    pick = (ids[:, None] == block_iota[None, :]).astype(half)
    sent = jnp.dot(pick, table, preferred_element_type=jnp.float32).astype(half)
    units = swap(sent.reshape(CHIPS, UNITS, ROWS * LANES), "chip")
    units = units.reshape(CHIPS, UNITS, ROWS, LANES).transpose(1, 2, 0, 3)
    units = units.reshape(UNITS, BLOCK, LANES)

    edges = jnp.stack([chip == 0, chip == CHIPS - 1]).astype(jnp.int32)
    outs, unit_grad, own_grad = vmem_call(
        attend_kernel,
        (
            jax.ShapeDtypeStruct((COLUMN, BLOCK, LANES), half),
            jax.ShapeDtypeStruct((UNITS, BLOCK, LANES), half),
            jax.ShapeDtypeStruct((COLUMN, BLOCK, LANES), jnp.float32),
        ),
        [pltpu.VMEM((2, BLOCK, LANES), jnp.float32)],
        in_specs=[pl.BlockSpec(memory_space=pltpu.SMEM)] + [pl.BlockSpec(memory_space=pltpu.VMEM)] * 2,
    )(edges, own, units)

    back = unit_grad.reshape(UNITS, ROWS, CHIPS, LANES).transpose(2, 0, 1, 3)
    back = swap(back.reshape(CHIPS, UNITS, ROWS * LANES), "chip").reshape(-1, ROWS * LANES)
    place = (block_iota[:, None] == ids[None, :]).astype(half)
    total = jnp.dot(place, back, preferred_element_type=jnp.float32).astype(half)
    total = swap(total.reshape(CHIPS, COLUMN, ROWS * LANES), "chip")
    total = total.reshape(CHIPS, COLUMN, ROWS, LANES).transpose(1, 2, 0, 3)
    total = total.reshape(COLUMN, BLOCK, LANES).astype(jnp.float32)
    pair_grad = (own_grad + total).astype(half)
    result = swap(jnp.concatenate([outs, pair_grad], axis=1), column)
    return vmem_call(unpack_kernel, (jax.ShapeDtypeStruct(query_rows.shape, half),) * 4)(result)


def solution(mesh):
    columns = Mesh(mesh.devices.reshape(CHIPS, 2, COLUMN // 2), ("chip", "core", "head"))
    rows = P(("chip", "core", "head"), None)
    return jax.shard_map(
        body,
        mesh=columns,
        in_specs=(rows, rows, rows, rows, P(("chip", "core"), None), P()),
        out_specs=(rows, rows, rows, rows),
        check_vma=False,
    )
```

time: 585 us -> 157 us (0.27)
  waiting for transfers between devices: 409 us -> 37.6 us
  blocking collectives: 0 us -> 67.4 us
  starting transfers between devices: 80.8 us -> 30.7 us
  local copies, waits for them, and re-layouts: 40.5 us -> 6.15 us
  between operations: 21.1 us -> 0.85 us
  other arithmetic: 19.5 us -> 1.1 us
  Pallas kernels: 0 us -> 11.1 us
  matrix products: 11.2 us -> 1.98 us
    psum x2 -> x0, waiting for transfers between devices: 325 us -> none  [the longest x1 172 us: broadcast(): return lax.psum(kept, axis)]
    all_to_all x0 -> x3, blocking collectives: none -> 67.4 us  [swap(): return lax.all_to_all(value, axis, split_axis=0, concat_axis=0, tiled=True)]
    all_to_all x11 -> x3, starting transfers between devices: 69.6 us -> 28.7 us  [swap(): return lax.all_to_all(value, axis, split_axis=0, concat_axis=0, tiled=True)]
    ppermute x4 -> x1, waiting for transfers between devices: 32.1 us -> 0.85 us  [body(): other = lax.ppermute(random_blocks, 'core', [(0, 1), (1, 0)])]
    all_to_all x11 -> x3, waiting for transfers between devices: 52.3 us -> 36.7 us  [swap(): return lax.all_to_all(value, axis, split_axis=0, concat_axis=0, tiled=True)]
    concatenate x5 -> x3, local copies, waits for them, and re-layouts: 14.2 us -> 0.25 us  [the longest x2 0.16 us: body(): jnp.concatenate([mine, other], 1)]
    pallas_call x0 -> x3, Pallas kernels: none -> 11.1 us  [the longest x1 9.16 us: body(): vmem_call(attend_kernel, (jax.ShapeDtypeStruct((COLUMN, BLOCK, LANES), ha...]
    all_to_all x9 -> x0, local copies, waits for them, and re-layouts: 9.74 us -> none  [the longest x1 1.58 us: body(): lax.all_to_all(key_rows, 'head', split_axis=1, concat_axis=0, tiled=True)]
  transfers between devices with their start and end apart: 17 -> 4, of which waited for: 11 -> 4; matrix products, arithmetic and copies ran while one was open for 10% -> 0% of each run, Pallas kernels for 0% -> 0%
where the time goes in v1:
time: 157 us
  blocking collectives  67.4 us (43%)
  waiting for transfers between devices  37.6 us (24%)
  starting transfers between devices  30.7 us (20%)
  Pallas kernels  11.1 us (7%)
  local copies, waits for them, and re-layouts  6.15 us (4%)
  matrix products  1.98 us (1%)
    all_to_all x3, blocking collectives, swap(): return lax.all_to_all(value, axis, split_axis=0, concat_axis=0, tiled=True)  67.4 us
    all_to_all x3, waiting for transfers between devices, swap(): return lax.all_to_all(value, axis, split_axis=0, concat_axis=0, tiled=True)  36.7 us
    all_to_all x3, starting transfers between devices, swap(): return lax.all_to_all(value, axis, split_axis=0, concat_axis=0, tiled=True)  28.7 us
    pallas_call x1, Pallas kernels, body(): vmem_call(attend_kernel, (jax.ShapeDtypeStruct((COLUMN, BLOCK, LANES), ha...  9.16 us
    unnamed x13, local copies, waits for them, and re-layouts  3.7 us
  transfers between devices with their start and end apart: 4, of which 4 were waited for; matrix products, arithmetic and copies ran while one was open for 0% of the time, Pallas kernels for 0%

profile of v1, /device:TPU:1, one launch (start us, length us, event | category | flops | bytes accessed | tf_op | source)
XLA Modules:
  0.0 156.9 jit_solution(18188969667826655246)
XLA Ops:
  0.6 0.9 copy-done
  1.5 0.9 copy-done.1
  2.4 0.9 copy-done.2
  3.3 0.9 copy-done.3
  4.3 1.0 shard_map.93
  5.3 12.0 %all-to-all-start = ((bf16[16,128,128]{2,1,0:T(8,128)(2,1)}), bf16[16,128,128]{2,1,0:T(8,128)(2,1)S(1)}, u32[]{:S(2)}, u32[]{:S(2)}) async-start(bf16[16,128,128]{2,1,0:T(8,128)(2,1)} %shard_map.93), calls=%async_computation | async-start | bytes 1048576 | tf_op jit(solution)/shard_map/all_to_all | solution.py:135
  17.2 2.0 %collective-permute-start = (s32[8,2]{0,1:T(2,128)S(1)}, s32[8,2]{0,1:T(2,128)S(1)}, u32[]{:S(2)}, u32[]{:S(2)}) collective-permute-start(s32[8,2]{0,1:T(2,128)S(1)} %copy-done.4), channel_id=1, source_target_pairs={{0,8},{8,0},{1,9},{9,1},{2,10},{10,2},{3,11},{11,3},{4,12},{12,4},... | collective-permute-start | bytes 200 | tf_op jit(solution)/shard_map/ppermute | solution.py:148
  19.4 0.8 collective-permute-done
  20.6 11.4 %all-to-all-done.own_ref = bf16[16,128,128]{2,1,0:T(8,128)(2,1)S(1)} async-done(((bf16[16,128,128]{2,1,0:T(8,128)(2,1)}), bf16[16,128,128]{2,1,0:T(8,128)(2,1)S(1)}, u32[]{:S(2)}, u32[]{:S(2)}) %all-to-all-start) | async-done | bytes 524320 | tf_op jit(solution)/shard_map/all_to_all | solution.py:135
  32.2 0.8 pad_maximum_fusion.1
  33.0 9.7 %all-to-all-start.1 = ((bf16[32,40,128]{2,1,0:T(8,128)(2,1)}), bf16[32,40,128]{2,1,0:T(8,128)(2,1)S(1)}, u32[]{:S(2)}, u32[]{:S(2)}) async-start(bf16[32,40,128]{2,1,0:T(8,128)(2,1)} %pad_maximum_fusion.1), calls=%async_computation.1 | async-start | bytes 655360 | tf_op jit(solution)/shard_map/all_to_all | solution.py:135
  42.7 9.9 %all-to-all-done.1 = bf16[32,40,128]{2,1,0:T(8,128)(2,1)S(1)} async-done(((bf16[32,40,128]{2,1,0:T(8,128)(2,1)}), bf16[32,40,128]{2,1,0:T(8,128)(2,1)S(1)}, u32[]{:S(2)}, u32[]{:S(2)}) %all-to-all-start.1) | async-done | bytes 327712 | tf_op jit(solution)/shard_map/all_to_all | solution.py:135
  52.9 1.4 fusion.2
  54.4 7.1 %all-to-all-start.2 = ((bf16[32,40,256]{2,1,0:T(8,128)(2,1)}), bf16[32,40,256]{2,1,0:T(8,128)(2,1)S(1)}, u32[]{:S(2)}, u32[]{:S(2)}) async-start(bf16[32,40,256]{2,1,0:T(8,128)(2,1)} %bitcast.8), calls=%async_computation.2 | async-start | bytes 1310720 | tf_op jit(solution)/shard_map/all_to_all | solution.py:135
  61.6 15.3 %all-to-all-done.2 = bf16[32,40,256]{2,1,0:T(8,128)(2,1)S(1)} async-done(((bf16[32,40,256]{2,1,0:T(8,128)(2,1)}), bf16[32,40,256]{2,1,0:T(8,128)(2,1)S(1)}, u32[]{:S(2)}, u32[]{:S(2)}) %all-to-all-start.2) | async-done | bytes 655392 | tf_op jit(solution)/shard_map/all_to_all | solution.py:135
  77.2 9.2 %shard_map.94 = (bf16[16,64,128]{2,1,0:T(8,128)(2,1)S(1)}, bf16[40,64,128]{2,1,0:T(8,128)(2,1)S(1)}, f32[16,64,128]{2,1,0:T(8,128)S(1)}) custom-call(s32[2]{0:T(128)S(1)} %add_convert_fusion.edge_ref, bf16[16,128,128]{2,1,0:T(8,128)(2,1)S(1)} %all-to-all-done.own_ref, bf16[40,64,128]{2,1,0:T(8,128)(2,1)S(1)} %bitcast.24), custom_call_target="tpu_custom_call" | custom-call | tf_op jit(solution)/shard_map/pallas_call | solution.py:187
  86.4 0.5 copy.19
  86.9 0.4 reshape.277
  87.3 22.2 %all_to_all.30 = bf16[32,40,256]{2,1,0:T(8,128)(2,1)S(1)} all-to-all(bf16[32,40,256]{2,1,0:T(8,128)(2,1)S(1)} %reshape.277), channel_id=1, replica_groups=mesh['chip'=32,'core'=2,'head'=8] {'chip'}, dimensions={0} | all-to-all | bytes 1310720 | tf_op jit(solution)/shard_map/all_to_all | solution.py:135
  109.6 0.5 fusion.5
  110.1 17.8 %all_to_all.31 = bf16[32,16,256]{2,1,0:T(8,128)(2,1)S(1)} all-to-all(bf16[32,16,256]{2,1,0:T(8,128)(2,1)S(1)} %bitcast.32), channel_id=1, replica_groups=mesh['chip'=32,'core'=2,'head'=8] {'chip'}, dimensions={0} | all-to-all | bytes 524288 | tf_op jit(solution)/shard_map/all_to_all | solution.py:135
  128.2 0.3 copy.17
  128.6 27.4 %all_to_all.32.in_ref = bf16[16,128,128]{2,1,0:T(8,128)(2,1)S(1)} all-to-all(bf16[16,128,128]{2,1,0:T(8,128)(2,1)S(1)} %pad_maximum_fusion), channel_id=1, replica_groups=mesh['chip'=32,'core'=2,'head'=8] {'core','head'}, dimensions={0} | all-to-all | bytes 1048576 | tf_op jit(solution)/shard_map/all_to_all | solution.py:135
  156.0 0.9 shard_map.95
  (32 shorter events, 1.7 us)
Async XLA Ops:
  0.6 0.9 copy-start
  1.5 0.9 copy-start.1
  2.4 0.9 copy-start.2
  3.3 0.9 copy-start.3
  5.3 12.0 %copy-start.4 = (s32[8,2]{0,1:T(2,128)S(1)}, s32[8,2]{0,1:T(2,128)}, u32[]{:S(2)}) copy-start(s32[8,2]{0,1:T(2,128)} %param.10) | copy-start | bytes 196
  5.3 26.7 %all-to-all-start = ((bf16[16,128,128]{2,1,0:T(8,128)(2,1)}), bf16[16,128,128]{2,1,0:T(8,128)(2,1)S(1)}, u32[]{:S(2)}, u32[]{:S(2)}) async-start(bf16[16,128,128]{2,1,0:T(8,128)(2,1)} %shard_map.93), calls=%async_computation | async-start | bytes 1048576 | tf_op jit(solution)/shard_map/all_to_all | solution.py:135
  17.2 3.0 %collective-permute-start = (s32[8,2]{0,1:T(2,128)S(1)}, s32[8,2]{0,1:T(2,128)S(1)}, u32[]{:S(2)}, u32[]{:S(2)}) collective-permute-start(s32[8,2]{0,1:T(2,128)S(1)} %copy-done.4), channel_id=1, source_target_pairs={{0,8},{8,0},{1,9},{9,1},{2,10},{10,2},{3,11},{11,3},{4,12},{12,4},... | collective-permute-start | bytes 200 | tf_op jit(solution)/shard_map/ppermute | solution.py:148
  32.2 20.5 %copy-start.5 = (s32[2]{0:T(128)S(1)}, s32[2]{0:T(128)}, u32[]{:S(2)}) copy-start(s32[2]{0:T(128)} %param.11) | copy-start | bytes 28
  33.0 19.6 %all-to-all-start.1 = ((bf16[32,40,128]{2,1,0:T(8,128)(2,1)}), bf16[32,40,128]{2,1,0:T(8,128)(2,1)S(1)}, u32[]{:S(2)}, u32[]{:S(2)}) async-start(bf16[32,40,128]{2,1,0:T(8,128)(2,1)} %pad_maximum_fusion.1), calls=%async_computation.1 | async-start | bytes 655360 | tf_op jit(solution)/shard_map/all_to_all | solution.py:135
  54.4 22.5 %all-to-all-start.2 = ((bf16[32,40,256]{2,1,0:T(8,128)(2,1)}), bf16[32,40,256]{2,1,0:T(8,128)(2,1)S(1)}, u32[]{:S(2)}, u32[]{:S(2)}) async-start(bf16[32,40,256]{2,1,0:T(8,128)(2,1)} %bitcast.8), calls=%async_computation.2 | async-start | bytes 1310720 | tf_op jit(solution)/shard_map/all_to_all | solution.py:135

commit v2 on v1

v2 whole, which is shorter than its diff:
```python
import math

import jax
import jax.numpy as jnp
from jax import lax
from jax.experimental import pallas as pl
from jax.experimental.pallas import tpu as pltpu
from jax.sharding import Mesh
from jax.sharding import PartitionSpec as P

HEAD_DIM = 64
BLOCK = 64
LANES = 128
COLUMN = 16
COLUMNS = 32
RANDOMS = 32
PARTNER = RANDOMS + 2
EDGE = PARTNER + COLUMN
USED = EDGE + 4
UNITS = 56
ROWS = 2
ID_ROWS = 8
GROUP = 8
SCALE = HEAD_DIM**-0.5
EXP2_SCALE = SCALE * math.log2(math.e)
VMEM = 48 * 1024 * 1024
WHOLE_VMEM = 60 * 1024 * 1024


def vmem_call(kernel, out_shape, scratch=(), vmem=VMEM, **specs):
    return pl.pallas_call(
        kernel,
        out_shape=out_shape,
        scratch_shapes=scratch,
        compiler_params=pltpu.CompilerParams(vmem_limit_bytes=vmem),
        **specs,
    )


def low_lanes(shape):
    return lax.broadcasted_iota(jnp.int32, shape, len(shape) - 1) < HEAD_DIM


def pack_kernel(random_ref, q_ref, g_ref, k_ref, v_ref, out_ref, held, arrived):
    copies = [
        pltpu.make_async_copy(ref, held.at[i], arrived.at[i])
        for i, ref in enumerate((q_ref, g_ref, k_ref, v_ref))
    ]
    for copy in copies:
        copy.start()
    yh, zh, zl = (lax.axis_index(axis) for axis in ("yh", "zh", "zl"))
    low = low_lanes((BLOCK, LANES))
    lane = lax.broadcasted_iota(jnp.int32, (ID_ROWS, LANES), 1)
    ids = jnp.zeros((ID_ROWS, LANES), jnp.int32)
    for step in range(2):
        name = random_ref[step, 2 * zh + zl]
        at = 2 * (4 * yh + zh) + step
        ids = jnp.where(lane == at, lax.shift_right_logical(name, 3), ids)
        ids = jnp.where(lane == at + RANDOMS, jnp.bitwise_and(name, 7), ids)
    ids = ids.astype(jnp.float32).astype(jnp.bfloat16)
    for rank in range(COLUMN):
        out_ref[rank, 2 * BLOCK :, :] = ids
    for row in range(2):
        copies[2 * row].wait()
        copies[2 * row + 1].wait()
        rows = slice(row * BLOCK, (row + 1) * BLOCK)
        for pair in range(COLUMN // 2):
            lanes = slice(pair * LANES, (pair + 1) * LANES)
            a = held[2 * row, :, lanes].astype(jnp.float32)
            b = held[2 * row + 1, :, lanes].astype(jnp.float32)
            a_turned = pltpu.roll(a, HEAD_DIM, 1)
            b_turned = pltpu.roll(b, HEAD_DIM, 1)
            out_ref[2 * pair, rows, :] = jnp.where(low, a, b_turned).astype(jnp.bfloat16)
            out_ref[2 * pair + 1, rows, :] = jnp.where(low, a_turned, b).astype(jnp.bfloat16)


def unpack_kernel(in_ref, o_ref, dq_ref, dk_ref, dv_ref):
    low = low_lanes((BLOCK, LANES))
    for row, (a_ref, b_ref) in enumerate(((dq_ref, o_ref), (dk_ref, dv_ref))):
        rows = slice(row * BLOCK, (row + 1) * BLOCK)
        for pair in range(COLUMN // 2):
            lanes = slice(pair * LANES, (pair + 1) * LANES)
            even = in_ref[2 * pair, rows, :].astype(jnp.float32)
            odd = in_ref[2 * pair + 1, rows, :].astype(jnp.float32)
            even_turned = pltpu.roll(even, HEAD_DIM, 1)
            odd_turned = pltpu.roll(odd, HEAD_DIM, 1)
            a_ref[:, lanes] = jnp.where(low, even, odd_turned).astype(jnp.bfloat16)
            b_ref[:, lanes] = jnp.where(low, even_turned, odd).astype(jnp.bfloat16)


def attend_kernel(flag_ref, own_ref, unit_ref, out_ref, grad_ref, own_grad_ref, shared, near, far):
    low = low_lanes((BLOCK, LANES))
    key_low = low_lanes((7 * BLOCK, LANES))
    far_keys = lax.broadcasted_iota(jnp.int32, (1, 7 * BLOCK), 1) // BLOCK == 2
    zero = jnp.zeros((BLOCK, LANES), jnp.bfloat16)
    odd = flag_ref[2] != 0
    shared[...] = jnp.zeros(shared.shape, jnp.float32)

    def far_key(block):
        before = block - 1 + PARTNER if block % 4 > 0 else EDGE + block // 4
        after = block + 1 + PARTNER if block % 4 < 3 else EDGE + block // 4
        return jnp.where(odd, unit_ref[after], unit_ref[before])

    for start in range(0, COLUMN, GROUP):
        group = range(start, start + GROUP)
        rows, keys, both, stacked = {}, {}, {}, {}
        for block in group:
            pair = own_ref[block, :BLOCK, :]
            rows[block] = jnp.concatenate(
                [jnp.where(low, pair, zero), jnp.where(low, zero, pair)], axis=0
            )
            keys[block] = jnp.concatenate(
                [
                    own_ref[block, BLOCK : 2 * BLOCK, :],
                    unit_ref[PARTNER + block],
                    far_key(block),
                    unit_ref[2 * block],
                    unit_ref[2 * block + 1],
                    unit_ref[RANDOMS],
                    unit_ref[RANDOMS + 1],
                ],
                axis=0,
            )
            both[block] = lax.dot_general(
                rows[block],
                keys[block],
                (((1,), (1,)), ((), ())),
                preferred_element_type=jnp.float32,
            )
        for block in group:
            scores, prob_grad = both[block][:BLOCK], both[block][BLOCK:]
            if block == 0:
                scores = jnp.where(far_keys & (flag_ref[0] != 0), -1e30, scores)
            if block == COLUMN - 1:
                scores = jnp.where(far_keys & (flag_ref[1] != 0), -1e30, scores)
            raised = jnp.exp2((scores - jnp.max(scores, axis=1, keepdims=True)) * EXP2_SCALE)
            probabilities = raised * (1.0 / jnp.sum(raised, axis=1, keepdims=True))
            probs_half = probabilities.astype(jnp.bfloat16)
            row_delta = jnp.sum(probs_half.astype(jnp.float32) * prob_grad, axis=1, keepdims=True)
            score_grad = (probabilities * (prob_grad - row_delta)).astype(jnp.bfloat16)
            stacked[block] = jnp.concatenate([score_grad, probs_half], axis=0)
        for block in group:
            mixed = jnp.dot(stacked[block], keys[block], preferred_element_type=jnp.float32)
            out_ref[block] = jnp.where(low, mixed[:BLOCK] * SCALE, mixed[BLOCK:]).astype(
                jnp.bfloat16
            )
            part = lax.dot_general(
                stacked[block],
                rows[block],
                (((0,), (0,)), ((), ())),
                preferred_element_type=jnp.float32,
            )
            part = jnp.where(key_low, part * SCALE, part)
            own_grad_ref[block] = part[:BLOCK]
            near[block] = part[BLOCK : 2 * BLOCK]
            far[block] = part[2 * BLOCK : 3 * BLOCK]
            for step in range(2):
                grad_ref[2 * block + step] = part[(3 + step) * BLOCK : (4 + step) * BLOCK].astype(
                    jnp.bfloat16
                )
                shared[step] += part[(5 + step) * BLOCK : (6 + step) * BLOCK]
    for step in range(2):
        grad_ref[RANDOMS + step] = shared[step].astype(jnp.bfloat16)
    none = jnp.zeros((BLOCK, LANES), jnp.float32)
    for block in range(COLUMN):
        after = far[block + 1] if block % 4 < 3 else none
        before = far[block - 1] if block % 4 > 0 else none
        grad_ref[PARTNER + block] = (near[block] + jnp.where(odd, before, after)).astype(
            jnp.bfloat16
        )
    for run in range(4):
        edge = jnp.where(odd, far[4 * run + 3], far[4 * run])
        grad_ref[EDGE + run] = edge.astype(jnp.bfloat16)
    for unit in range(USED, UNITS):
        grad_ref[unit] = zero


def swap(value, axis):
    return lax.all_to_all(value, axis, split_axis=0, concat_axis=0, tiled=True)


def body(query_rows, key_rows, value_rows, out_grad, random_blocks, global_blocks):
    half = jnp.bfloat16
    column, plane = ("yh", "zh"), ("x", "yl", "zl", "core")
    blocks = COLUMNS * COLUMN
    odd = lax.axis_index("zl")
    my_column = lax.axis_index(plane)

    columns = jnp.arange(COLUMNS, dtype=jnp.int32)[:, None]
    places = jnp.arange(COLUMN, dtype=jnp.int32)[None]
    numbers = (
        columns // 8 * 128
        + columns // 4 % 2 * 16
        + columns % 2 * 8
        + columns // 2 % 2
        + places // 4 * 32
        + places % 4 * 2
    )
    odd_column = columns // 2 % 2
    partners = numbers + 1 - 2 * odd_column
    edges = jnp.where(odd_column == 1, numbers[:, 3::4] + 1, numbers[:, 0::4] - 1)

    smem, hbm = pl.BlockSpec(memory_space=pltpu.SMEM), pl.BlockSpec(memory_space=pltpu.HBM)
    vmem = pl.BlockSpec(memory_space=pltpu.VMEM)
    packed = vmem_call(
        pack_kernel,
        jax.ShapeDtypeStruct((COLUMN, 2 * BLOCK + ID_ROWS, LANES), half),
        [pltpu.VMEM((4, *query_rows.shape), half), pltpu.SemaphoreType.DMA((4,))],
        vmem=WHOLE_VMEM,
        in_specs=[smem] + [hbm] * 4,
    )(random_blocks.T, query_rows, out_grad, key_rows, value_rows)
    own = swap(packed, column)

    spread = own[:, BLOCK : 2 * BLOCK].reshape(COLUMN, ROWS, COLUMNS, LANES).transpose(2, 1, 0, 3)
    spread = spread.reshape(COLUMNS, ROWS * COLUMN, LANES)
    named = jnp.sum(own[:, 2 * BLOCK :].astype(jnp.float32), axis=0).astype(half)
    named = jnp.broadcast_to(named[None], (COLUMNS, ID_ROWS, LANES))
    held = swap(jnp.concatenate([spread, named], axis=1), plane)

    table = jnp.concatenate(
        [held[:, r * COLUMN : (r + 1) * COLUMN].reshape(blocks, LANES) for r in range(ROWS)], axis=1
    )
    ids = held[:, ROWS * COLUMN, : 2 * RANDOMS].astype(jnp.float32)
    ids = (ids[:, :RANDOMS] * 8 + ids[:, RANDOMS:]).astype(jnp.int32)
    shared = jnp.broadcast_to(global_blocks[None], (COLUMNS, 2))
    unused = jnp.full((COLUMNS, UNITS - USED), -1, jnp.int32)
    ids = jnp.concatenate([ids, shared, partners, edges, unused], axis=1).reshape(-1)
    numbers = numbers.reshape(-1)
    pick = (ids[:, None] == numbers[None, :]).astype(half)
    sent = jnp.dot(pick, table, preferred_element_type=jnp.float32).astype(half)
    units = swap(sent.reshape(COLUMNS, UNITS, ROWS * LANES), plane)
    units = units.reshape(COLUMNS, UNITS, ROWS, LANES).transpose(1, 2, 0, 3)
    units = units.reshape(UNITS, BLOCK, LANES)

    flags = jnp.stack([my_column == 0, my_column == COLUMNS - 1, odd == 1]).astype(jnp.int32)
    outs, unit_grad, own_grad = vmem_call(
        attend_kernel,
        (
            jax.ShapeDtypeStruct((COLUMN, BLOCK, LANES), half),
            jax.ShapeDtypeStruct((UNITS, BLOCK, LANES), half),
            jax.ShapeDtypeStruct((COLUMN, BLOCK, LANES), jnp.float32),
        ),
        [pltpu.VMEM((count, BLOCK, LANES), jnp.float32) for count in (2, COLUMN, COLUMN)],
        in_specs=[smem, vmem, vmem],
    )(flags, own, units)

    back = unit_grad.reshape(UNITS, ROWS, COLUMNS, LANES).transpose(2, 0, 1, 3)
    back = swap(back.reshape(COLUMNS, UNITS, ROWS * LANES), plane).reshape(-1, ROWS * LANES)
    place = (numbers[:, None] == ids[None, :]).astype(half)
    total = jnp.dot(place, back, preferred_element_type=jnp.float32).astype(half)
    total = swap(total.reshape(COLUMNS, COLUMN, ROWS * LANES), plane)
    total = total.reshape(COLUMNS, COLUMN, ROWS, LANES).transpose(1, 2, 0, 3)
    total = total.reshape(COLUMN, BLOCK, LANES).astype(jnp.float32)
    pair_grad = (own_grad + total).astype(half)
    result = swap(jnp.concatenate([outs, pair_grad], axis=1), column)
    return vmem_call(unpack_kernel, (jax.ShapeDtypeStruct(query_rows.shape, half),) * 4)(result)


def solution(mesh):
    split = Mesh(
        mesh.devices.reshape(4, 4, 2, 2, 4, 2), ("x", "yh", "yl", "core", "zh", "zl")
    )
    seq = ("x", "yh", "yl", "core")
    rows = P((*seq, "zh", "zl"), None)
    return jax.shard_map(
        body,
        mesh=split,
        in_specs=(rows, rows, rows, rows, P(seq, None), P()),
        out_specs=(rows, rows, rows, rows),
        check_vma=False,
    )
```

time: 157 us -> 142 us (0.904)
  blocking collectives: 67.4 us -> 55.6 us
  waiting for transfers between devices: 37.6 us -> 45.1 us
  Pallas kernels: 11.1 us -> 6.67 us
  starting transfers between devices: 30.7 us -> 26.5 us
  local copies, waits for them, and re-layouts: 6.15 us -> 2.96 us
    all_to_all x3, blocking collectives: 67.4 us -> 55.6 us  [swap(): return lax.all_to_all(value, axis, split_axis=0, concat_axis=0, tiled=True)]
    all_to_all x3, waiting for transfers between devices: 36.7 us -> 45.1 us  [swap(): return lax.all_to_all(value, axis, split_axis=0, concat_axis=0, tiled=True)]
    pallas_call x1, Pallas kernels: 9.16 us -> 2.96 us  [body(): vmem_call(attend_kernel, (jax.ShapeDtypeStruct((COLUMN, BLOCK, LANES), ha...]
    unnamed x13 -> x2, local copies, waits for them, and re-layouts: 3.7 us -> 0.01 us
    all_to_all x3, starting transfers between devices: 28.7 us -> 26.5 us  [swap(): return lax.all_to_all(value, axis, split_axis=0, concat_axis=0, tiled=True)]
    ppermute x1 -> x0, starting transfers between devices: 2.01 us -> none  [body(): other = lax.ppermute(random_blocks, 'core', [(0, 1), (1, 0)])]
    pallas_call x1, Pallas kernels: 1.02 us -> 2.77 us  [body(): vmem_call(pack_kernel, jax.ShapeDtypeStruct((COLUMN, 2 * BLOCK + ID_ROWS,...]
  transfers between devices with their start and end apart: 4 -> 3, of which waited for: 4 -> 3; matrix products, arithmetic and copies ran while one was open for 0% -> 0% of each run, Pallas kernels for 0% -> 0%
where the time goes in v2:
time: 142 us; the launch traced here: 141 us
  blocking collectives  55.6 us (39%)
  waiting for transfers between devices  45.1 us (32%)
  starting transfers between devices  26.5 us (19%)
  Pallas kernels  6.67 us (5%)
  local copies, waits for them, and re-layouts  2.96 us (2%)
  matrix products  2.4 us (2%)
    all_to_all x3, blocking collectives, swap(): return lax.all_to_all(value, axis, split_axis=0, concat_axis=0, tiled=True)  55.6 us
    all_to_all x3, waiting for transfers between devices, swap(): return lax.all_to_all(value, axis, split_axis=0, concat_axis=0, tiled=True)  45.1 us
    all_to_all x3, starting transfers between devices, swap(): return lax.all_to_all(value, axis, split_axis=0, concat_axis=0, tiled=True)  26.5 us
    pallas_call x1, Pallas kernels, body(): vmem_call(attend_kernel, (jax.ShapeDtypeStruct((COLUMN, BLOCK, LANES), ha...  2.96 us
  transfers between devices with their start and end apart: 3, of which 3 were waited for; matrix products, arithmetic and copies ran while one was open for 0% of the time, Pallas kernels for 0%

profile of v2, /device:TPU:1, one launch (start us, length us, event | category | flops | bytes accessed | tf_op | source)
XLA Modules:
  0.0 141.2 jit_solution(17616356003084551229)
XLA Ops:
  0.6 2.8 %shard_map.93 = bf16[16,136,128]{2,1,0:T(8,128)(2,1)} custom-call(s32[2,8]{1,0:T(2,128)} %bitcast.38, bf16[64,1024]{1,0:T(8,128)(2,1)} %q_ref.1, bf16[64,1024]{1,0:T(8,128)(2,1)} %g_ref.1, bf16[64,1024]{1,0:T(8,128)(2,1)} %k_ref.1, bf16[64,1024]{1,0:T(8,128)(2,1)} %v_ref.1), custom_call_target="tpu_custom_call" | custom-call | tf_op jit(solution)/shard_map/pallas_call | solution.py:205
  3.4 16.2 %all-to-all-start = ((bf16[16,136,128]{2,1,0:T(8,128)(2,1)}), bf16[16,136,128]{2,1,0:T(8,128)(2,1)S(1)}, u32[]{:S(2)}, u32[]{:S(2)}) async-start(bf16[16,136,128]{2,1,0:T(8,128)(2,1)} %shard_map.93), calls=%async_computation | async-start | bytes 1114112 | tf_op jit(solution)/shard_map/all_to_all | solution.py:179
  19.7 21.2 %all-to-all-done.own_ref = bf16[16,136,128]{2,1,0:T(8,128)(2,1)S(1)} async-done(((bf16[16,136,128]{2,1,0:T(8,128)(2,1)}), bf16[16,136,128]{2,1,0:T(8,128)(2,1)S(1)}, u32[]{:S(2)}, u32[]{:S(2)}) %all-to-all-start) | async-done | bytes 557088 | tf_op jit(solution)/shard_map/all_to_all | solution.py:179
  40.8 0.2 copy.10
  41.1 0.7 pad_maximum_fusion.1
  41.8 6.5 %all-to-all-start.1 = ((bf16[32,40,128]{2,1,0:T(8,128)(2,1)}), bf16[32,40,128]{2,1,0:T(8,128)(2,1)S(1)}, u32[]{:S(2)}, u32[]{:S(2)}) async-start(bf16[32,40,128]{2,1,0:T(8,128)(2,1)} %pad_maximum_fusion.1), calls=%async_computation.1 | async-start | bytes 655360 | tf_op jit(solution)/shard_map/all_to_all | solution.py:179
  48.6 0.1 slice.32
  48.8 8.6 %all-to-all-done.1 = bf16[32,40,128]{2,1,0:T(8,128)(2,1)S(1)} async-done(((bf16[32,40,128]{2,1,0:T(8,128)(2,1)}), bf16[32,40,128]{2,1,0:T(8,128)(2,1)S(1)}, u32[]{:S(2)}, u32[]{:S(2)}) %all-to-all-start.1) | async-done | bytes 327712 | tf_op jit(solution)/shard_map/all_to_all | solution.py:179
  57.6 0.1 eq.57
  57.7 1.7 %fusion.4 = bf16[1792,256]{1,0:T(8,128)(2,1)} fusion(s32[512]{0:T(512)S(1)} %add.261, s32[1792]{0:T(1024)S(1)} %eq.57, bf16[512,128]{1,0:T(8,128)(2,1)S(1)} %bitcast.37, bf16[512,128]{1,0:T(8,128)(2,1)S(1)} %bitcast.36), kind=kOutput, calls=%fused_computation.4 | convolution fusion | flops 471662592 | bytes 1188864 | tf_op jit(solution)/shard_map/dot_general | solution.py:230
  59.4 3.7 %all-to-all-start.2 = ((bf16[32,56,256]{2,1,0:T(8,128)(2,1)}), bf16[32,56,256]{2,1,0:T(8,128)(2,1)S(1)}, u32[]{:S(2)}, u32[]{:S(2)}) async-start(bf16[32,56,256]{2,1,0:T(8,128)(2,1)} %bitcast.10), calls=%async_computation.2 | async-start | bytes 1835008 | tf_op jit(solution)/shard_map/all_to_all | solution.py:179
  63.2 15.3 %all-to-all-done.2 = bf16[32,56,256]{2,1,0:T(8,128)(2,1)S(1)} async-done(((bf16[32,56,256]{2,1,0:T(8,128)(2,1)}), bf16[32,56,256]{2,1,0:T(8,128)(2,1)S(1)}, u32[]{:S(2)}, u32[]{:S(2)}) %all-to-all-start.2) | async-done | bytes 917536 | tf_op jit(solution)/shard_map/all_to_all | solution.py:179
  78.5 0.2 reshape.321
  78.7 0.2 copy.11
  79.0 3.0 %shard_map.94 = (bf16[16,64,128]{2,1,0:T(8,128)(2,1)S(1)}, bf16[56,64,128]{2,1,0:T(8,128)(2,1)S(1)}, f32[16,64,128]{2,1,0:T(8,128)S(1)}) custom-call(s32[3]{0:T(128)S(1)} %add_convert_fusion.flag_ref, bf16[16,136,128]{2,1,0:T(8,128)(2,1)S(1)} %all-to-all-done.own_ref, bf16[56,64,128]{2,1,0:T(8,128)(2,1)S(1)} %bitcast.26), custom_call_target="tpu_custom_call" | custom-call | tf_op jit(solution)/shard_map/pallas_call | solution.py:236
  81.9 0.7 copy.15
  82.7 0.6 reshape.324
  83.3 18.8 %all_to_all.30 = bf16[32,56,256]{2,1,0:T(8,128)(2,1)S(1)} all-to-all(bf16[32,56,256]{2,1,0:T(8,128)(2,1)S(1)} %reshape.324), channel_id=1, replica_groups=mesh['x'=4,'yh'=4,'yl'=2,'core'=2,'zh'=4,'zl'=2] {'x','yl','zl','core'}, dimensions={0} | all-to-all | bytes 1835008 | tf_op jit(solution)/shard_map/all_to_all | solution.py:179
  102.1 0.7 fusion.11
  102.8 11.8 %all_to_all.31 = bf16[32,16,256]{2,1,0:T(8,128)(2,1)S(1)} all-to-all(bf16[32,16,256]{2,1,0:T(8,128)(2,1)S(1)} %bitcast.34), channel_id=1, replica_groups=mesh['x'=4,'yh'=4,'yl'=2,'core'=2,'zh'=4,'zl'=2] {'x','yl','zl','core'}, dimensions={0} | all-to-all | bytes 524288 | tf_op jit(solution)/shard_map/all_to_all | solution.py:179
  114.7 0.3 reshape.329
  114.9 0.3 copy.13
  115.4 24.9 %all_to_all.32.in_ref = bf16[16,128,128]{2,1,0:T(8,128)(2,1)S(1)} all-to-all(bf16[16,128,128]{2,1,0:T(8,128)(2,1)S(1)} %pad_maximum_fusion), channel_id=1, replica_groups=mesh['x'=4,'yh'=4,'yl'=2,'core'=2,'zh'=4,'zl'=2] {'yh','zh'}, dimensions={0} | all-to-all | bytes 1048576 | tf_op jit(solution)/shard_map/all_to_all | solution.py:179
  140.3 0.9 shard_map.95
  (21 shorter events, 0.8 us)
Async XLA Ops:
  3.4 37.4 %all-to-all-start = ((bf16[16,136,128]{2,1,0:T(8,128)(2,1)}), bf16[16,136,128]{2,1,0:T(8,128)(2,1)S(1)}, u32[]{:S(2)}, u32[]{:S(2)}) async-start(bf16[16,136,128]{2,1,0:T(8,128)(2,1)} %shard_map.93), calls=%async_computation | async-start | bytes 1114112 | tf_op jit(solution)/shard_map/all_to_all | solution.py:179
  41.0 16.5 %copy-start = (s32[2]{0:T(128)S(1)}, s32[2]{0:T(128)}, u32[]{:S(2)}) copy-start(s32[2]{0:T(128)} %param.11) | copy-start | bytes 28
  41.8 15.6 %all-to-all-start.1 = ((bf16[32,40,128]{2,1,0:T(8,128)(2,1)}), bf16[32,40,128]{2,1,0:T(8,128)(2,1)S(1)}, u32[]{:S(2)}, u32[]{:S(2)}) async-start(bf16[32,40,128]{2,1,0:T(8,128)(2,1)} %pad_maximum_fusion.1), calls=%async_computation.1 | async-start | bytes 655360 | tf_op jit(solution)/shard_map/all_to_all | solution.py:179
  59.4 19.1 %all-to-all-start.2 = ((bf16[32,56,256]{2,1,0:T(8,128)(2,1)}), bf16[32,56,256]{2,1,0:T(8,128)(2,1)S(1)}, u32[]{:S(2)}, u32[]{:S(2)}) async-start(bf16[32,56,256]{2,1,0:T(8,128)(2,1)} %bitcast.10), calls=%async_computation.2 | async-start | bytes 1835008 | tf_op jit(solution)/shard_map/all_to_all | solution.py:179

commit v3 on v2

--- a/solution.py
+++ b/solution.py
@@ -41,19 +41,22 @@
     return lax.broadcasted_iota(jnp.int32, shape, len(shape) - 1) < HEAD_DIM
 
 
-def pack_kernel(random_ref, q_ref, g_ref, k_ref, v_ref, out_ref, held, arrived):
+def pack_kernel(random_ref, q_ref, g_ref, k_ref, v_ref, out_ref, held, named, arrived):
+    names = pltpu.make_async_copy(random_ref, named, arrived.at[4])
     copies = [
         pltpu.make_async_copy(ref, held.at[i], arrived.at[i])
         for i, ref in enumerate((q_ref, g_ref, k_ref, v_ref))
     ]
+    names.start()
     for copy in copies:
         copy.start()
     yh, zh, zl = (lax.axis_index(axis) for axis in ("yh", "zh", "zl"))
     low = low_lanes((BLOCK, LANES))
     lane = lax.broadcasted_iota(jnp.int32, (ID_ROWS, LANES), 1)
     ids = jnp.zeros((ID_ROWS, LANES), jnp.int32)
+    names.wait()
     for step in range(2):
-        name = random_ref[step, 2 * zh + zl]
+        name = named[step, 2 * zh + zl]
         at = 2 * (4 * yh + zh) + step
         ids = jnp.where(lane == at, lax.shift_right_logical(name, 3), ids)
         ids = jnp.where(lane == at + RANDOMS, jnp.bitwise_and(name, 7), ids)
@@ -205,9 +208,13 @@
     packed = vmem_call(
         pack_kernel,
         jax.ShapeDtypeStruct((COLUMN, 2 * BLOCK + ID_ROWS, LANES), half),
-        [pltpu.VMEM((4, *query_rows.shape), half), pltpu.SemaphoreType.DMA((4,))],
+        [
+            pltpu.VMEM((4, *query_rows.shape), half),
+            pltpu.SMEM(random_blocks.shape[::-1], jnp.int32),
+            pltpu.SemaphoreType.DMA((5,)),
+        ],
         vmem=WHOLE_VMEM,
-        in_specs=[smem] + [hbm] * 4,
+        in_specs=[hbm] * 5,
     )(random_blocks.T, query_rows, out_grad, key_rows, value_rows)
     own = swap(packed, column)
 
@@ -244,12 +251,21 @@
         in_specs=[smem, vmem, vmem],
     )(flags, own, units)
 
-    back = unit_grad.reshape(UNITS, ROWS, COLUMNS, LANES).transpose(2, 0, 1, 3)
-    back = swap(back.reshape(COLUMNS, UNITS, ROWS * LANES), plane).reshape(-1, ROWS * LANES)
+    back = unit_grad.reshape(UNITS, ROWS, COLUMNS, LANES).transpose(2, 1, 0, 3)
+    back = swap(back.reshape(COLUMNS, ROWS * UNITS, LANES), plane)
     place = (numbers[:, None] == ids[None, :]).astype(half)
-    total = jnp.dot(place, back, preferred_element_type=jnp.float32).astype(half)
-    total = swap(total.reshape(COLUMNS, COLUMN, ROWS * LANES), plane)
-    total = total.reshape(COLUMNS, COLUMN, ROWS, LANES).transpose(1, 2, 0, 3)
+    total = [
+        jnp.dot(
+            place,
+            back[:, r * UNITS : (r + 1) * UNITS].reshape(-1, LANES),
+            preferred_element_type=jnp.float32,
+        )
+        .astype(half)
+        .reshape(COLUMNS, COLUMN, LANES)
+        for r in range(ROWS)
+    ]
+    total = swap(jnp.concatenate(total, axis=1), plane)
+    total = total.reshape(COLUMNS, ROWS, COLUMN, LANES).transpose(2, 1, 0, 3)
     total = total.reshape(COLUMN, BLOCK, LANES).astype(jnp.float32)
     pair_grad = (own_grad + total).astype(half)
     result = swap(jnp.concatenate([outs, pair_grad], axis=1), column)

time: 142 us -> 141 us (level)
  no operation moved by 1% of the time
where the time goes in v3:
time: 141 us; the launch traced here: 140 us
  blocking collectives  55.6 us (39%)
  waiting for transfers between devices  45.1 us (32%)
  starting transfers between devices  26.5 us (19%)
  Pallas kernels  6.02 us (4%)
  matrix products  3.09 us (2%)
  local copies, waits for them, and re-layouts  2.08 us (1%)
    all_to_all x3, blocking collectives, swap(): return lax.all_to_all(value, axis, split_axis=0, concat_axis=0, tiled=True)  55.6 us
    all_to_all x3, waiting for transfers between devices, swap(): return lax.all_to_all(value, axis, split_axis=0, concat_axis=0, tiled=True)  45.1 us
    all_to_all x3, starting transfers between devices, swap(): return lax.all_to_all(value, axis, split_axis=0, concat_axis=0, tiled=True)  26.5 us
    pallas_call x1, Pallas kernels, body(): vmem_call(attend_kernel, (jax.ShapeDtypeStruct((COLUMN, BLOCK, LANES), ha...  2.96 us
  transfers between devices with their start and end apart: 3, of which 3 were waited for; matrix products, arithmetic and copies ran while one was open for 0% of the time, Pallas kernels for 0%

profile of v3, /device:TPU:1, one launch (start us, length us, event | category | flops | bytes accessed | tf_op | source)
XLA Modules:
  0.0 140.5 jit_solution(14597895369953418806)
XLA Ops:
  0.6 2.1 %shard_map.93 = bf16[16,136,128]{2,1,0:T(8,128)(2,1)} custom-call(s32[2,8]{1,0:T(2,128)} %bitcast.46, bf16[64,1024]{1,0:T(8,128)(2,1)} %q_ref.1, bf16[64,1024]{1,0:T(8,128)(2,1)} %g_ref.1, bf16[64,1024]{1,0:T(8,128)(2,1)} %k_ref.1, bf16[64,1024]{1,0:T(8,128)(2,1)} %v_ref.1), custom_call_target="tpu_custom_call" | custom-call | tf_op jit(solution)/shard_map/pallas_call | solution.py:208
  2.7 16.2 %all-to-all-start = ((bf16[16,136,128]{2,1,0:T(8,128)(2,1)}), bf16[16,136,128]{2,1,0:T(8,128)(2,1)S(1)}, u32[]{:S(2)}, u32[]{:S(2)}) async-start(bf16[16,136,128]{2,1,0:T(8,128)(2,1)} %shard_map.93), calls=%async_computation | async-start | bytes 1114112 | tf_op jit(solution)/shard_map/all_to_all | solution.py:182
  19.0 21.2 %all-to-all-done.own_ref = bf16[16,136,128]{2,1,0:T(8,128)(2,1)S(1)} async-done(((bf16[16,136,128]{2,1,0:T(8,128)(2,1)}), bf16[16,136,128]{2,1,0:T(8,128)(2,1)S(1)}, u32[]{:S(2)}, u32[]{:S(2)}) %all-to-all-start) | async-done | bytes 557088 | tf_op jit(solution)/shard_map/all_to_all | solution.py:182
  40.2 0.2 copy.10
  40.4 0.8 pad_maximum_fusion.1
  41.2 6.5 %all-to-all-start.1 = ((bf16[32,40,128]{2,1,0:T(8,128)(2,1)}), bf16[32,40,128]{2,1,0:T(8,128)(2,1)S(1)}, u32[]{:S(2)}, u32[]{:S(2)}) async-start(bf16[32,40,128]{2,1,0:T(8,128)(2,1)} %pad_maximum_fusion.1), calls=%async_computation.1 | async-start | bytes 655360 | tf_op jit(solution)/shard_map/all_to_all | solution.py:182
  47.9 0.1 slice.38
  48.1 8.6 %all-to-all-done.1 = bf16[32,40,128]{2,1,0:T(8,128)(2,1)S(1)} async-done(((bf16[32,40,128]{2,1,0:T(8,128)(2,1)}), bf16[32,40,128]{2,1,0:T(8,128)(2,1)S(1)}, u32[]{:S(2)}, u32[]{:S(2)}) %all-to-all-start.1) | async-done | bytes 327712 | tf_op jit(solution)/shard_map/all_to_all | solution.py:182
  56.8 0.1 concatenate.16
  56.9 0.1 eq.57
  57.0 1.7 %fusion.6 = bf16[1792,256]{1,0:T(8,128)(2,1)} fusion(s32[512]{0:T(512)S(1)} %add.261, s32[1792]{0:T(1024)S(1)} %eq.57, bf16[512,128]{1,0:T(8,128)(2,1)S(1)} %bitcast.45, bf16[512,128]{1,0:T(8,128)(2,1)S(1)} %bitcast.44), kind=kOutput, calls=%fused_computation.6 | convolution fusion | flops 471662592 | bytes 1188864 | tf_op jit(solution)/shard_map/dot_general | solution.py:237
  58.7 3.7 %all-to-all-start.2 = ((bf16[32,56,256]{2,1,0:T(8,128)(2,1)}), bf16[32,56,256]{2,1,0:T(8,128)(2,1)S(1)}, u32[]{:S(2)}, u32[]{:S(2)}) async-start(bf16[32,56,256]{2,1,0:T(8,128)(2,1)} %bitcast.10), calls=%async_computation.2 | async-start | bytes 1835008 | tf_op jit(solution)/shard_map/all_to_all | solution.py:182
  62.5 15.3 %all-to-all-done.2 = bf16[32,56,256]{2,1,0:T(8,128)(2,1)S(1)} async-done(((bf16[32,56,256]{2,1,0:T(8,128)(2,1)}), bf16[32,56,256]{2,1,0:T(8,128)(2,1)S(1)}, u32[]{:S(2)}, u32[]{:S(2)}) %all-to-all-start.2) | async-done | bytes 917536 | tf_op jit(solution)/shard_map/all_to_all | solution.py:182
  77.9 0.2 reshape.327
  78.1 0.2 copy.11
  78.3 3.0 %shard_map.94 = (bf16[16,64,128]{2,1,0:T(8,128)(2,1)S(1)}, bf16[56,64,128]{2,1,0:T(8,128)(2,1)S(1)}, f32[16,64,128]{2,1,0:T(8,128)S(1)}) custom-call(s32[3]{0:T(128)S(1)} %add_convert_fusion.flag_ref, bf16[16,136,128]{2,1,0:T(8,128)(2,1)S(1)} %all-to-all-done.own_ref, bf16[56,64,128]{2,1,0:T(8,128)(2,1)S(1)} %bitcast.32), custom_call_target="tpu_custom_call" | custom-call | tf_op jit(solution)/shard_map/pallas_call | solution.py:243
  81.3 0.6 copy.12
  81.9 18.8 %all_to_all.30 = bf16[32,112,128]{2,1,0:T(8,128)(2,1)S(1)} all-to-all(bf16[32,112,128]{2,1,0:T(8,128)(2,1)S(1)} %bitcast.35), channel_id=1, replica_groups=mesh['x'=4,'yh'=4,'yl'=2,'core'=2,'zh'=4,'zl'=2] {'x','yl','zl','core'}, dimensions={0} | all-to-all | bytes 1835008 | tf_op jit(solution)/shard_map/all_to_all | solution.py:182
  100.8 0.7 fusion.15
  101.5 0.7 fusion.18
  102.2 11.8 %all_to_all.31 = bf16[32,32,128]{2,1,0:T(8,128)(2,1)S(1)} all-to-all(bf16[32,32,128]{2,1,0:T(8,128)(2,1)S(1)} %pad_maximum_fusion.2), channel_id=1, replica_groups=mesh['x'=4,'yh'=4,'yl'=2,'core'=2,'zh'=4,'zl'=2] {'x','yl','zl','core'}, dimensions={0} | all-to-all | bytes 524288 | tf_op jit(solution)/shard_map/all_to_all | solution.py:182
  114.2 0.3 copy.13
  114.6 25.0 %all_to_all.32.in_ref = bf16[16,128,128]{2,1,0:T(8,128)(2,1)S(1)} all-to-all(bf16[16,128,128]{2,1,0:T(8,128)(2,1)S(1)} %pad_maximum_fusion), channel_id=1, replica_groups=mesh['x'=4,'yh'=4,'yl'=2,'core'=2,'zh'=4,'zl'=2] {'yh','zh'}, dimensions={0} | all-to-all | bytes 1048576 | tf_op jit(solution)/shard_map/all_to_all | solution.py:182
  139.5 0.9 shard_map.95
  (23 shorter events, 0.8 us)
Async XLA Ops:
  2.7 37.4 %all-to-all-start = ((bf16[16,136,128]{2,1,0:T(8,128)(2,1)}), bf16[16,136,128]{2,1,0:T(8,128)(2,1)S(1)}, u32[]{:S(2)}, u32[]{:S(2)}) async-start(bf16[16,136,128]{2,1,0:T(8,128)(2,1)} %shard_map.93), calls=%async_computation | async-start | bytes 1114112 | tf_op jit(solution)/shard_map/all_to_all | solution.py:182
  40.4 16.5 %copy-start = (s32[2]{0:T(128)S(1)}, s32[2]{0:T(128)}, u32[]{:S(2)}) copy-start(s32[2]{0:T(128)} %param.11) | copy-start | bytes 28
  41.2 15.6 %all-to-all-start.1 = ((bf16[32,40,128]{2,1,0:T(8,128)(2,1)}), bf16[32,40,128]{2,1,0:T(8,128)(2,1)S(1)}, u32[]{:S(2)}, u32[]{:S(2)}) async-start(bf16[32,40,128]{2,1,0:T(8,128)(2,1)} %pad_maximum_fusion.1), calls=%async_computation.1 | async-start | bytes 655360 | tf_op jit(solution)/shard_map/all_to_all | solution.py:182
  58.7 19.1 %all-to-all-start.2 = ((bf16[32,56,256]{2,1,0:T(8,128)(2,1)}), bf16[32,56,256]{2,1,0:T(8,128)(2,1)S(1)}, u32[]{:S(2)}, u32[]{:S(2)}) async-start(bf16[32,56,256]{2,1,0:T(8,128)(2,1)} %bitcast.10), calls=%async_computation.2 | async-start | bytes 1835008 | tf_op jit(solution)/shard_map/all_to_all | solution.py:182

commit v4 on v3

--- a/solution.py
+++ b/solution.py
@@ -2,6 +2,7 @@
 
 import jax
 import jax.numpy as jnp
+import numpy as np
 from jax import lax
 from jax.experimental import pallas as pl
 from jax.experimental.pallas import tpu as pltpu
@@ -91,12 +92,14 @@
             b_ref[:, lanes] = jnp.where(low, even_turned, odd).astype(jnp.bfloat16)
 
 
-def attend_kernel(flag_ref, own_ref, unit_ref, out_ref, grad_ref, own_grad_ref, shared, near, far):
+def attend_kernel(own_ref, unit_ref, out_ref, grad_ref, own_grad_ref, shared, near, far):
     low = low_lanes((BLOCK, LANES))
     key_low = low_lanes((7 * BLOCK, LANES))
     far_keys = lax.broadcasted_iota(jnp.int32, (1, 7 * BLOCK), 1) // BLOCK == 2
     zero = jnp.zeros((BLOCK, LANES), jnp.bfloat16)
-    odd = flag_ref[2] != 0
+    x, yl, zl, core = (lax.axis_index(axis) for axis in ("x", "yl", "zl", "core"))
+    column = 8 * x + 4 * yl + 2 * zl + core
+    odd = zl == 1
     shared[...] = jnp.zeros(shared.shape, jnp.float32)
 
     def far_key(block):
@@ -133,9 +136,9 @@
         for block in group:
             scores, prob_grad = both[block][:BLOCK], both[block][BLOCK:]
             if block == 0:
-                scores = jnp.where(far_keys & (flag_ref[0] != 0), -1e30, scores)
+                scores = jnp.where(far_keys & (column == 0), -1e30, scores)
             if block == COLUMN - 1:
-                scores = jnp.where(far_keys & (flag_ref[1] != 0), -1e30, scores)
+                scores = jnp.where(far_keys & (column == COLUMNS - 1), -1e30, scores)
             raised = jnp.exp2((scores - jnp.max(scores, axis=1, keepdims=True)) * EXP2_SCALE)
             probabilities = raised * (1.0 / jnp.sum(raised, axis=1, keepdims=True))
             probs_half = probabilities.astype(jnp.bfloat16)
@@ -186,11 +189,9 @@
     half = jnp.bfloat16
     column, plane = ("yh", "zh"), ("x", "yl", "zl", "core")
     blocks = COLUMNS * COLUMN
-    odd = lax.axis_index("zl")
-    my_column = lax.axis_index(plane)
-
-    columns = jnp.arange(COLUMNS, dtype=jnp.int32)[:, None]
-    places = jnp.arange(COLUMN, dtype=jnp.int32)[None]
+
+    columns = np.arange(COLUMNS, dtype=np.int32)[:, None]
+    places = np.arange(COLUMN, dtype=np.int32)[None]
     numbers = (
         columns // 8 * 128
         + columns // 4 % 2 * 16
@@ -201,9 +202,9 @@
     )
     odd_column = columns // 2 % 2
     partners = numbers + 1 - 2 * odd_column
-    edges = jnp.where(odd_column == 1, numbers[:, 3::4] + 1, numbers[:, 0::4] - 1)
-
-    smem, hbm = pl.BlockSpec(memory_space=pltpu.SMEM), pl.BlockSpec(memory_space=pltpu.HBM)
+    edges = np.where(odd_column == 1, numbers[:, 3::4] + 1, numbers[:, 0::4] - 1)
+
+    hbm = pl.BlockSpec(memory_space=pltpu.HBM)
     vmem = pl.BlockSpec(memory_space=pltpu.VMEM)
     packed = vmem_call(
         pack_kernel,
@@ -224,14 +225,16 @@
     named = jnp.broadcast_to(named[None], (COLUMNS, ID_ROWS, LANES))
     held = swap(jnp.concatenate([spread, named], axis=1), plane)
 
+    held, global_blocks = lax.optimization_barrier((held, global_blocks))
     table = jnp.concatenate(
         [held[:, r * COLUMN : (r + 1) * COLUMN].reshape(blocks, LANES) for r in range(ROWS)], axis=1
     )
     ids = held[:, ROWS * COLUMN, : 2 * RANDOMS].astype(jnp.float32)
     ids = (ids[:, :RANDOMS] * 8 + ids[:, RANDOMS:]).astype(jnp.int32)
     shared = jnp.broadcast_to(global_blocks[None], (COLUMNS, 2))
-    unused = jnp.full((COLUMNS, UNITS - USED), -1, jnp.int32)
-    ids = jnp.concatenate([ids, shared, partners, edges, unused], axis=1).reshape(-1)
+    unused = np.full((COLUMNS, UNITS - USED), -1, np.int32)
+    fixed = np.concatenate([partners, edges, unused], axis=1)
+    ids = jnp.concatenate([ids, shared, fixed], axis=1).reshape(-1)
     numbers = numbers.reshape(-1)
     pick = (ids[:, None] == numbers[None, :]).astype(half)
     sent = jnp.dot(pick, table, preferred_element_type=jnp.float32).astype(half)
@@ -239,7 +242,6 @@
     units = units.reshape(COLUMNS, UNITS, ROWS, LANES).transpose(1, 2, 0, 3)
     units = units.reshape(UNITS, BLOCK, LANES)
 
-    flags = jnp.stack([my_column == 0, my_column == COLUMNS - 1, odd == 1]).astype(jnp.int32)
     outs, unit_grad, own_grad = vmem_call(
         attend_kernel,
         (
@@ -248,8 +250,8 @@
             jax.ShapeDtypeStruct((COLUMN, BLOCK, LANES), jnp.float32),
         ),
         [pltpu.VMEM((count, BLOCK, LANES), jnp.float32) for count in (2, COLUMN, COLUMN)],
-        in_specs=[smem, vmem, vmem],
-    )(flags, own, units)
+        in_specs=[vmem, vmem],
+    )(own, units)
 
     back = unit_grad.reshape(UNITS, ROWS, COLUMNS, LANES).transpose(2, 1, 0, 3)
     back = swap(back.reshape(COLUMNS, ROWS * UNITS, LANES), plane)

time: 141 us -> 138 us (0.979)
  blocking collectives: 55.6 us -> 127 us
  waiting for transfers between devices: 45.1 us -> 0 us
  starting transfers between devices: 26.5 us -> 0 us
    all_to_all x3 -> x6, blocking collectives: 55.6 us -> 127 us  [swap(): return lax.all_to_all(value, axis, split_axis=0, concat_axis=0, tiled=True)]
    all_to_all x3 -> x0, waiting for transfers between devices: 45.1 us -> none  [swap(): return lax.all_to_all(value, axis, split_axis=0, concat_axis=0, tiled=True)]
    all_to_all x3 -> x0, starting transfers between devices: 26.5 us -> none  [swap(): return lax.all_to_all(value, axis, split_axis=0, concat_axis=0, tiled=True)]
  transfers between devices with their start and end apart: 3 -> 0, of which waited for: 3 -> 0; matrix products, arithmetic and copies ran while one was open for 0% -> 0% of each run, Pallas kernels for 0% -> 0%
where the time goes in v4:
time: 138 us
  blocking collectives  127 us (92%)
  Pallas kernels  5.46 us (4%)
  matrix products  2.15 us (2%)
  local copies, waits for them, and re-layouts  1.83 us (1%)
    all_to_all x6, blocking collectives, swap(): return lax.all_to_all(value, axis, split_axis=0, concat_axis=0, tiled=True)  127 us

profile of v4, /device:TPU:1, one launch (start us, length us, event | category | flops | bytes accessed | tf_op | source)
XLA Modules:
  0.0 138.0 jit_solution(398009348531602674)
XLA Ops:
  0.6 2.1 %shard_map.120 = bf16[16,136,128]{2,1,0:T(8,128)(2,1)} custom-call(s32[2,8]{1,0:T(2,128)} %bitcast.44, bf16[64,1024]{1,0:T(8,128)(2,1)} %q_ref.1, bf16[64,1024]{1,0:T(8,128)(2,1)} %g_ref.1, bf16[64,1024]{1,0:T(8,128)(2,1)} %k_ref.1, bf16[64,1024]{1,0:T(8,128)(2,1)} %v_ref.1), custom_call_target="tpu_custom_call" | custom-call | tf_op jit(solution)/shard_map/pallas_call | solution.py:209
  2.7 38.1 %all_to_all.30.own_ref = bf16[16,136,128]{2,1,0:T(8,128)(2,1)S(1)} all-to-all(bf16[16,136,128]{2,1,0:T(8,128)(2,1)} %shard_map.120), channel_id=1, replica_groups=mesh['x'=4,'yh'=4,'yl'=2,'core'=2,'zh'=4,'zl'=2] {'yh','zh'}, dimensions={0} | all-to-all | bytes 1114112 | tf_op jit(solution)/shard_map/all_to_all | solution.py:185
  40.8 0.2 copy.13
  41.1 0.0 copy-start
  41.1 15.5 %all_to_all.31 = bf16[32,40,128]{2,1,0:T(8,128)(2,1)S(1)} all-to-all(bf16[32,40,128]{2,1,0:T(8,128)(2,1)S(1)} %pad_maximum_fusion.1), channel_id=1, replica_groups=mesh['x'=4,'yh'=4,'yl'=2,'core'=2,'zh'=4,'zl'=2] {'x','yl','zl','core'}, dimensions={0} | all-to-all | bytes 655360 | tf_op jit(solution)/shard_map/all_to_all | solution.py:185
  56.6 0.1 fusion.25
  56.7 0.1 pad.7.clone
  56.8 0.1 pad_add_fusion
  56.9 0.1 eq.32
  57.0 0.8 fusion.6
  57.7 18.7 %all_to_all.32 = bf16[32,56,256]{2,1,0:T(8,128)(2,1)S(1)} all-to-all(bf16[32,56,256]{2,1,0:T(8,128)(2,1)S(1)} %bitcast.36), channel_id=1, replica_groups=mesh['x'=4,'yh'=4,'yl'=2,'core'=2,'zh'=4,'zl'=2] {'x','yl','zl','core'}, dimensions={0} | all-to-all | bytes 1835008 | tf_op jit(solution)/shard_map/all_to_all | solution.py:185
  76.4 0.2 reshape.64
  76.6 0.2 copy.14
  76.9 2.4 %shard_map.121 = (bf16[16,64,128]{2,1,0:T(8,128)(2,1)S(1)}, bf16[56,64,128]{2,1,0:T(8,128)(2,1)S(1)}, f32[16,64,128]{2,1,0:T(8,128)S(1)}) custom-call(bf16[16,136,128]{2,1,0:T(8,128)(2,1)S(1)} %all_to_all.30.own_ref, bf16[56,64,128]{2,1,0:T(8,128)(2,1)S(1)} %bitcast.29), custom_call_target="tpu_custom_call" | custom-call | tf_op jit(solution)/shard_map/pallas_call | solution.py:245
  79.3 0.6 copy.15
  79.9 18.9 %all_to_all.33 = bf16[32,112,128]{2,1,0:T(8,128)(2,1)S(1)} all-to-all(bf16[32,112,128]{2,1,0:T(8,128)(2,1)S(1)} %bitcast.32), channel_id=1, replica_groups=mesh['x'=4,'yh'=4,'yl'=2,'core'=2,'zh'=4,'zl'=2] {'x','yl','zl','core'}, dimensions={0} | all-to-all | bytes 1835008 | tf_op jit(solution)/shard_map/all_to_all | solution.py:185
  98.8 0.1 fusion.27
  98.9 0.7 fusion.15
  99.6 0.7 fusion.18
  100.3 11.8 %all_to_all.34 = bf16[32,32,128]{2,1,0:T(8,128)(2,1)S(1)} all-to-all(bf16[32,32,128]{2,1,0:T(8,128)(2,1)S(1)} %pad_maximum_fusion.2), channel_id=1, replica_groups=mesh['x'=4,'yh'=4,'yl'=2,'core'=2,'zh'=4,'zl'=2] {'x','yl','zl','core'}, dimensions={0} | all-to-all | bytes 524288 | tf_op jit(solution)/shard_map/all_to_all | solution.py:185
  112.2 0.3 copy.16
  112.5 0.1 fusion.21
  112.6 24.4 %all_to_all.35.in_ref = bf16[16,128,128]{2,1,0:T(8,128)(2,1)S(1)} all-to-all(bf16[16,128,128]{2,1,0:T(8,128)(2,1)S(1)} %pad_maximum_fusion), channel_id=1, replica_groups=mesh['x'=4,'yh'=4,'yl'=2,'core'=2,'zh'=4,'zl'=2] {'yh','zh'}, dimensions={0} | all-to-all | bytes 1048576 | tf_op jit(solution)/shard_map/all_to_all | solution.py:185
  137.0 0.9 shard_map.122
  (14 shorter events, 0.2 us)
Async XLA Ops:
  41.0 15.7 %copy-start.1 = (s32[2]{0:T(128)S(1)}, s32[2]{0:T(128)}, u32[]{:S(2)}) copy-start(s32[2]{0:T(128)} %param.14) | copy-start | bytes 28
  41.1 15.7 %copy-start = (s32[32,22]{1,0:T(8,128)S(1)}, s32[32,22]{1,0:T(8,128)}, u32[]{:S(2)}) copy-start(s32[32,22]{1,0:T(8,128)} %constant.11.clone) | copy-start | bytes 8452
  41.1 15.9 %copy-start.2 = (s32[512]{0:T(512)S(1)}, s32[512]{0:T(512)}, u32[]{:S(2)}) copy-start(s32[512]{0:T(512)} %constant.19) | copy-start | bytes 6148

commit v5 on v4

--- a/solution.py
+++ b/solution.py
@@ -42,15 +42,23 @@
     return lax.broadcasted_iota(jnp.int32, shape, len(shape) - 1) < HEAD_DIM
 
 
-def pack_kernel(random_ref, q_ref, g_ref, k_ref, v_ref, out_ref, held, named, arrived):
-    names = pltpu.make_async_copy(random_ref, named, arrived.at[4])
-    copies = [
-        pltpu.make_async_copy(ref, held.at[i], arrived.at[i])
-        for i, ref in enumerate((q_ref, g_ref, k_ref, v_ref))
-    ]
+def pack_kernel(random_ref, q_ref, g_ref, k_ref, v_ref, out_ref, held, named, packed, arrived, left):
+    names = pltpu.make_async_copy(random_ref, named, arrived.at[8])
     names.start()
-    for copy in copies:
-        copy.start()
+    width, heads = held.shape[-1] // 2, COLUMN // 2
+    copies, leaving = [], []
+    for half in range(2):
+        lanes = pl.ds(half * width, width)
+        for i, ref in enumerate((q_ref, g_ref, k_ref, v_ref)):
+            copy = pltpu.make_async_copy(
+                ref.at[:, lanes], held.at[i, :, lanes], arrived.at[4 * half + i]
+            )
+            copy.start()
+            copies.append(copy)
+        ranks = pl.ds(half * heads, heads)
+        leaving.append(
+            pltpu.make_async_copy(packed.at[ranks], out_ref.at[ranks], left.at[half])
+        )
     yh, zh, zl = (lax.axis_index(axis) for axis in ("yh", "zh", "zl"))
     low = low_lanes((BLOCK, LANES))
     lane = lax.broadcasted_iota(jnp.int32, (ID_ROWS, LANES), 1)
@@ -63,19 +71,23 @@
         ids = jnp.where(lane == at + RANDOMS, jnp.bitwise_and(name, 7), ids)
     ids = ids.astype(jnp.float32).astype(jnp.bfloat16)
     for rank in range(COLUMN):
-        out_ref[rank, 2 * BLOCK :, :] = ids
-    for row in range(2):
-        copies[2 * row].wait()
-        copies[2 * row + 1].wait()
-        rows = slice(row * BLOCK, (row + 1) * BLOCK)
-        for pair in range(COLUMN // 2):
+        packed[rank, 2 * BLOCK :, :] = ids
+    for half in range(2):
+        for copy in copies[4 * half : 4 * half + 4]:
+            copy.wait()
+        for pair in range(half * heads // 2, (half + 1) * heads // 2):
             lanes = slice(pair * LANES, (pair + 1) * LANES)
-            a = held[2 * row, :, lanes].astype(jnp.float32)
-            b = held[2 * row + 1, :, lanes].astype(jnp.float32)
-            a_turned = pltpu.roll(a, HEAD_DIM, 1)
-            b_turned = pltpu.roll(b, HEAD_DIM, 1)
-            out_ref[2 * pair, rows, :] = jnp.where(low, a, b_turned).astype(jnp.bfloat16)
-            out_ref[2 * pair + 1, rows, :] = jnp.where(low, a_turned, b).astype(jnp.bfloat16)
+            for row in range(2):
+                rows = slice(row * BLOCK, (row + 1) * BLOCK)
+                a = held[2 * row, :, lanes].astype(jnp.float32)
+                b = held[2 * row + 1, :, lanes].astype(jnp.float32)
+                a_turned = pltpu.roll(a, HEAD_DIM, 1)
+                b_turned = pltpu.roll(b, HEAD_DIM, 1)
+                packed[2 * pair, rows, :] = jnp.where(low, a, b_turned).astype(jnp.bfloat16)
+                packed[2 * pair + 1, rows, :] = jnp.where(low, a_turned, b).astype(jnp.bfloat16)
+        leaving[half].start()
+    for copy in leaving:
+        copy.wait()
 
 
 def unpack_kernel(in_ref, o_ref, dq_ref, dk_ref, dv_ref):
@@ -212,10 +224,13 @@
         [
             pltpu.VMEM((4, *query_rows.shape), half),
             pltpu.SMEM(random_blocks.shape[::-1], jnp.int32),
-            pltpu.SemaphoreType.DMA((5,)),
+            pltpu.VMEM((COLUMN, 2 * BLOCK + ID_ROWS, LANES), half),
+            pltpu.SemaphoreType.DMA((9,)),
+            pltpu.SemaphoreType.DMA((2,)),
         ],
         vmem=WHOLE_VMEM,
         in_specs=[hbm] * 5,
+        out_specs=hbm,
     )(random_blocks.T, query_rows, out_grad, key_rows, value_rows)
     own = swap(packed, column)
 
@@ -253,21 +268,12 @@
         in_specs=[vmem, vmem],
     )(own, units)
 
-    back = unit_grad.reshape(UNITS, ROWS, COLUMNS, LANES).transpose(2, 1, 0, 3)
-    back = swap(back.reshape(COLUMNS, ROWS * UNITS, LANES), plane)
+    back = unit_grad.reshape(UNITS, ROWS, COLUMNS, LANES).transpose(2, 0, 1, 3)
+    back = swap(back.reshape(COLUMNS, UNITS, ROWS * LANES), plane).reshape(-1, ROWS * LANES)
     place = (numbers[:, None] == ids[None, :]).astype(half)
-    total = [
-        jnp.dot(
-            place,
-            back[:, r * UNITS : (r + 1) * UNITS].reshape(-1, LANES),
-            preferred_element_type=jnp.float32,
-        )
-        .astype(half)
-        .reshape(COLUMNS, COLUMN, LANES)
-        for r in range(ROWS)
-    ]
-    total = swap(jnp.concatenate(total, axis=1), plane)
-    total = total.reshape(COLUMNS, ROWS, COLUMN, LANES).transpose(2, 1, 0, 3)
+    total = jnp.dot(place, back, preferred_element_type=jnp.float32).astype(half)
+    total = swap(total.reshape(COLUMNS, COLUMN, ROWS * LANES), plane)
+    total = total.reshape(COLUMNS, COLUMN, ROWS, LANES).transpose(1, 2, 0, 3)
     total = total.reshape(COLUMN, BLOCK, LANES).astype(jnp.float32)
     pair_grad = (own_grad + total).astype(half)
     result = swap(jnp.concatenate([outs, pair_grad], axis=1), column)

time: 138 us -> 138 us (level)
  no operation moved by 1% of the time
where the time goes in v5:
time: 138 us
  blocking collectives  127 us (92%)
  Pallas kernels  5.39 us (4%)
  local copies, waits for them, and re-layouts  2.71 us (2%)
  matrix products  1.45 us (1%)
    all_to_all x6, blocking collectives, swap(): return lax.all_to_all(value, axis, split_axis=0, concat_axis=0, tiled=True)  127 us

profile of v5, /device:TPU:1, one launch (start us, length us, event | category | flops | bytes accessed | tf_op | source)
XLA Modules:
  0.0 138.0 jit_solution(3504104377099005880)
XLA Ops:
  0.6 2.0 %shard_map.120 = bf16[16,136,128]{2,1,0:T(8,128)(2,1)} custom-call(s32[2,8]{1,0:T(2,128)} %bitcast.36, bf16[64,1024]{1,0:T(8,128)(2,1)} %q_ref.1, bf16[64,1024]{1,0:T(8,128)(2,1)} %g_ref.1, bf16[64,1024]{1,0:T(8,128)(2,1)} %k_ref.1, bf16[64,1024]{1,0:T(8,128)(2,1)} %v_ref.1), custom_call_target="tpu_custom_call" | custom-call | tf_op jit(solution)/shard_map/pallas_call | solution.py:221
  2.7 38.1 %all_to_all.30.own_ref = bf16[16,136,128]{2,1,0:T(8,128)(2,1)S(1)} all-to-all(bf16[16,136,128]{2,1,0:T(8,128)(2,1)} %shard_map.120), channel_id=1, replica_groups=mesh['x'=4,'yh'=4,'yl'=2,'core'=2,'zh'=4,'zl'=2] {'yh','zh'}, dimensions={0} | all-to-all | bytes 1114112 | tf_op jit(solution)/shard_map/all_to_all | solution.py:197
  40.8 0.2 copy.13
  41.0 0.0 copy-start.2
  41.0 15.5 %all_to_all.31 = bf16[32,40,128]{2,1,0:T(8,128)(2,1)S(1)} all-to-all(bf16[32,40,128]{2,1,0:T(8,128)(2,1)S(1)} %pad_maximum_fusion.1), channel_id=1, replica_groups=mesh['x'=4,'yh'=4,'yl'=2,'core'=2,'zh'=4,'zl'=2] {'x','yl','zl','core'}, dimensions={0} | all-to-all | bytes 655360 | tf_op jit(solution)/shard_map/all_to_all | solution.py:197
  56.6 0.1 fusion.18
  56.7 0.1 pad.5.clone
  56.7 0.1 pad_add_fusion
  56.8 0.1 eq.32
  56.9 0.8 fusion.4
  57.7 18.7 %all_to_all.32 = bf16[32,56,256]{2,1,0:T(8,128)(2,1)S(1)} all-to-all(bf16[32,56,256]{2,1,0:T(8,128)(2,1)S(1)} %bitcast.31), channel_id=1, replica_groups=mesh['x'=4,'yh'=4,'yl'=2,'core'=2,'zh'=4,'zl'=2] {'x','yl','zl','core'}, dimensions={0} | all-to-all | bytes 1835008 | tf_op jit(solution)/shard_map/all_to_all | solution.py:197
  76.4 0.2 reshape.58
  76.6 0.2 copy.14
  76.8 2.4 %shard_map.121 = (bf16[16,64,128]{2,1,0:T(8,128)(2,1)S(1)}, bf16[56,64,128]{2,1,0:T(8,128)(2,1)S(1)}, f32[16,64,128]{2,1,0:T(8,128)S(1)}) custom-call(bf16[16,136,128]{2,1,0:T(8,128)(2,1)S(1)} %all_to_all.30.own_ref, bf16[56,64,128]{2,1,0:T(8,128)(2,1)S(1)} %bitcast.23), custom_call_target="tpu_custom_call" | custom-call | tf_op jit(solution)/shard_map/pallas_call | solution.py:260
  79.2 0.7 copy.18
  80.0 0.6 reshape.61
  80.5 18.9 %all_to_all.33 = bf16[32,56,256]{2,1,0:T(8,128)(2,1)S(1)} all-to-all(bf16[32,56,256]{2,1,0:T(8,128)(2,1)S(1)} %reshape.61), channel_id=1, replica_groups=mesh['x'=4,'yh'=4,'yl'=2,'core'=2,'zh'=4,'zl'=2] {'x','yl','zl','core'}, dimensions={0} | all-to-all | bytes 1835008 | tf_op jit(solution)/shard_map/all_to_all | solution.py:197
  99.4 0.7 fusion.11
  100.1 11.8 %all_to_all.34 = bf16[32,16,256]{2,1,0:T(8,128)(2,1)S(1)} all-to-all(bf16[32,16,256]{2,1,0:T(8,128)(2,1)S(1)} %bitcast.32), channel_id=1, replica_groups=mesh['x'=4,'yh'=4,'yl'=2,'core'=2,'zh'=4,'zl'=2] {'x','yl','zl','core'}, dimensions={0} | all-to-all | bytes 524288 | tf_op jit(solution)/shard_map/all_to_all | solution.py:197
  112.0 0.3 reshape.66
  112.2 0.3 copy.16
  112.5 0.1 fusion.14
  112.7 24.4 %all_to_all.35.in_ref = bf16[16,128,128]{2,1,0:T(8,128)(2,1)S(1)} all-to-all(bf16[16,128,128]{2,1,0:T(8,128)(2,1)S(1)} %pad_maximum_fusion), channel_id=1, replica_groups=mesh['x'=4,'yh'=4,'yl'=2,'core'=2,'zh'=4,'zl'=2] {'yh','zh'}, dimensions={0} | all-to-all | bytes 1048576 | tf_op jit(solution)/shard_map/all_to_all | solution.py:197
  137.0 0.9 shard_map.122
  (12 shorter events, 0.2 us)
Async XLA Ops:
  41.0 15.7 %copy-start.1 = (s32[2]{0:T(128)S(1)}, s32[2]{0:T(128)}, u32[]{:S(2)}) copy-start(s32[2]{0:T(128)} %param.14) | copy-start | bytes 28
  41.0 15.7 %copy-start = (s32[32,22]{1,0:T(8,128)S(1)}, s32[32,22]{1,0:T(8,128)}, u32[]{:S(2)}) copy-start(s32[32,22]{1,0:T(8,128)} %constant.11.clone) | copy-start | bytes 8452
  41.0 15.9 %copy-start.2 = (s32[512]{0:T(512)S(1)}, s32[512]{0:T(512)}, u32[]{:S(2)}) copy-start(s32[512]{0:T(512)} %constant.19) | copy-start | bytes 6148

commit v6 on v4

--- a/solution.py
+++ b/solution.py
@@ -255,7 +255,8 @@
 
     back = unit_grad.reshape(UNITS, ROWS, COLUMNS, LANES).transpose(2, 1, 0, 3)
     back = swap(back.reshape(COLUMNS, ROWS * UNITS, LANES), plane)
-    place = (numbers[:, None] == ids[None, :]).astype(half)
+    ids, back = lax.optimization_barrier((ids, back))
+    place = lax.optimization_barrier((numbers[:, None] == ids[None, :]).astype(half))
     total = [
         jnp.dot(
             place,
@@ -268,7 +269,7 @@
     ]
     total = swap(jnp.concatenate(total, axis=1), plane)
     total = total.reshape(COLUMNS, ROWS, COLUMN, LANES).transpose(2, 1, 0, 3)
-    total = total.reshape(COLUMN, BLOCK, LANES).astype(jnp.float32)
+    total = lax.optimization_barrier(total.reshape(COLUMN, BLOCK, LANES)).astype(jnp.float32)
     pair_grad = (own_grad + total).astype(half)
     result = swap(jnp.concatenate([outs, pair_grad], axis=1), column)
     return vmem_call(unpack_kernel, (jax.ShapeDtypeStruct(query_rows.shape, half),) * 4)(result)

time: 138 us -> 138 us (level)
  no operation moved by 1% of the time
where the time goes in v6:
time: 138 us
  blocking collectives  127 us (92%)
  Pallas kernels  5.46 us (4%)
  matrix products  2.04 us (1%)
  local copies, waits for them, and re-layouts  1.62 us (1%)
    all_to_all x6, blocking collectives, swap(): return lax.all_to_all(value, axis, split_axis=0, concat_axis=0, tiled=True)  127 us

profile of v6, /device:TPU:1, one launch (start us, length us, event | category | flops | bytes accessed | tf_op | source)
XLA Modules:
  0.0 137.9 jit_solution(1880728467450635411)
XLA Ops:
  0.6 2.1 %shard_map.120 = bf16[16,136,128]{2,1,0:T(8,128)(2,1)} custom-call(s32[2,8]{1,0:T(2,128)} %bitcast.43, bf16[64,1024]{1,0:T(8,128)(2,1)} %q_ref.1, bf16[64,1024]{1,0:T(8,128)(2,1)} %g_ref.1, bf16[64,1024]{1,0:T(8,128)(2,1)} %k_ref.1, bf16[64,1024]{1,0:T(8,128)(2,1)} %v_ref.1), custom_call_target="tpu_custom_call" | custom-call | tf_op jit(solution)/shard_map/pallas_call | solution.py:209
  2.8 38.1 %all_to_all.30.own_ref = bf16[16,136,128]{2,1,0:T(8,128)(2,1)S(1)} all-to-all(bf16[16,136,128]{2,1,0:T(8,128)(2,1)} %shard_map.120), channel_id=1, replica_groups=mesh['x'=4,'yh'=4,'yl'=2,'core'=2,'zh'=4,'zl'=2] {'yh','zh'}, dimensions={0} | all-to-all | bytes 1114112 | tf_op jit(solution)/shard_map/all_to_all | solution.py:185
  40.9 0.2 copy.13
  41.1 15.5 %all_to_all.31 = bf16[32,40,128]{2,1,0:T(8,128)(2,1)S(1)} all-to-all(bf16[32,40,128]{2,1,0:T(8,128)(2,1)S(1)} %pad_maximum_fusion.1), channel_id=1, replica_groups=mesh['x'=4,'yh'=4,'yl'=2,'core'=2,'zh'=4,'zl'=2] {'x','yl','zl','core'}, dimensions={0} | all-to-all | bytes 655360 | tf_op jit(solution)/shard_map/all_to_all | solution.py:185
  56.6 0.1 fusion.10
  56.7 0.1 pad.7.clone
  56.8 0.1 pad_add_fusion
  56.9 0.1 eq.32
  57.0 0.8 fusion.2
  57.7 18.7 %all_to_all.32 = bf16[32,56,256]{2,1,0:T(8,128)(2,1)S(1)} all-to-all(bf16[32,56,256]{2,1,0:T(8,128)(2,1)S(1)} %bitcast.37), channel_id=1, replica_groups=mesh['x'=4,'yh'=4,'yl'=2,'core'=2,'zh'=4,'zl'=2] {'x','yl','zl','core'}, dimensions={0} | all-to-all | bytes 1835008 | tf_op jit(solution)/shard_map/all_to_all | solution.py:185
  76.4 0.2 reshape.65
  76.6 0.2 copy.14
  76.9 2.4 %shard_map.121 = (bf16[16,64,128]{2,1,0:T(8,128)(2,1)S(1)}, bf16[56,64,128]{2,1,0:T(8,128)(2,1)S(1)}, f32[16,64,128]{2,1,0:T(8,128)S(1)}) custom-call(bf16[16,136,128]{2,1,0:T(8,128)(2,1)S(1)} %all_to_all.30.own_ref, bf16[56,64,128]{2,1,0:T(8,128)(2,1)S(1)} %bitcast.27), custom_call_target="tpu_custom_call" | custom-call | tf_op jit(solution)/shard_map/pallas_call | solution.py:245
  79.3 0.6 copy.15
  79.9 18.9 %all_to_all.33 = bf16[32,112,128]{2,1,0:T(8,128)(2,1)S(1)} all-to-all(bf16[32,112,128]{2,1,0:T(8,128)(2,1)S(1)} %bitcast.30), channel_id=1, replica_groups=mesh['x'=4,'yh'=4,'yl'=2,'core'=2,'zh'=4,'zl'=2] {'x','yl','zl','core'}, dimensions={0} | all-to-all | bytes 1835008 | tf_op jit(solution)/shard_map/all_to_all | solution.py:185
  98.8 0.1 fusion.12
  98.9 0.4 compare_convert_fusion
  99.2 0.6 convolution_convert_fusion
  99.9 0.6 convolution_convert_fusion.1
  100.5 11.8 %all_to_all.34 = bf16[32,32,128]{2,1,0:T(8,128)(2,1)S(1)} all-to-all(bf16[32,32,128]{2,1,0:T(8,128)(2,1)S(1)} %pad_maximum_fusion.2), channel_id=1, replica_groups=mesh['x'=4,'yh'=4,'yl'=2,'core'=2,'zh'=4,'zl'=2] {'x','yl','zl','core'}, dimensions={0} | all-to-all | bytes 524288 | tf_op jit(solution)/shard_map/all_to_all | solution.py:185
  112.4 0.1 copy.16
  112.5 0.1 add_convert_fusion
  112.6 24.4 %all_to_all.35.in_ref = bf16[16,128,128]{2,1,0:T(8,128)(2,1)S(1)} all-to-all(bf16[16,128,128]{2,1,0:T(8,128)(2,1)S(1)} %pad_maximum_fusion), channel_id=1, replica_groups=mesh['x'=4,'yh'=4,'yl'=2,'core'=2,'zh'=4,'zl'=2] {'yh','zh'}, dimensions={0} | all-to-all | bytes 1048576 | tf_op jit(solution)/shard_map/all_to_all | solution.py:185
  137.0 0.9 shard_map.122
  (14 shorter events, 0.2 us)
Async XLA Ops:
  2.7 54.0 %copy-start.2 = (s32[2]{0:T(128)S(1)}, s32[2]{0:T(128)}, u32[]{:S(2)}) copy-start(s32[2]{0:T(128)} %param.14) | copy-start | bytes 28
  2.7 54.0 %copy-start = (s32[32,22]{1,0:T(8,128)S(1)}, s32[32,22]{1,0:T(8,128)}, u32[]{:S(2)}) copy-start(s32[32,22]{1,0:T(8,128)} %constant.11.clone) | copy-start | bytes 8452
  40.8 16.1 %copy-start.1 = (s32[512]{0:T(512)S(1)}, s32[512]{0:T(512)}, u32[]{:S(2)}) copy-start(s32[512]{0:T(512)} %constant.19) | copy-start | bytes 6148

commit v7 on v4

--- a/solution.py
+++ b/solution.py
@@ -98,7 +98,7 @@
     far_keys = lax.broadcasted_iota(jnp.int32, (1, 7 * BLOCK), 1) // BLOCK == 2
     zero = jnp.zeros((BLOCK, LANES), jnp.bfloat16)
     x, yl, zl, core = (lax.axis_index(axis) for axis in ("x", "yl", "zl", "core"))
-    column = 8 * x + 4 * yl + 2 * zl + core
+    column = 16 * zl + 8 * yl + 2 * x + core
     odd = zl == 1
     shared[...] = jnp.zeros(shared.shape, jnp.float32)
 
@@ -187,20 +187,20 @@
 
 def body(query_rows, key_rows, value_rows, out_grad, random_blocks, global_blocks):
     half = jnp.bfloat16
-    column, plane = ("yh", "zh"), ("x", "yl", "zl", "core")
+    column, plane = ("yh", "zh"), ("zl", "yl", "x", "core")
     blocks = COLUMNS * COLUMN
 
     columns = np.arange(COLUMNS, dtype=np.int32)[:, None]
     places = np.arange(COLUMN, dtype=np.int32)[None]
     numbers = (
-        columns // 8 * 128
-        + columns // 4 % 2 * 16
+        columns // 2 % 4 * 128
+        + columns // 8 % 2 * 16
         + columns % 2 * 8
-        + columns // 2 % 2
+        + columns // 16
         + places // 4 * 32
         + places % 4 * 2
     )
-    odd_column = columns // 2 % 2
+    odd_column = columns // 16
     partners = numbers + 1 - 2 * odd_column
     edges = np.where(odd_column == 1, numbers[:, 3::4] + 1, numbers[:, 0::4] - 1)
 

time: 138 us -> 138 us (level)
  no operation moved by 1% of the time
where the time goes in v7:
time: 138 us
  blocking collectives  127 us (92%)
  Pallas kernels  5.46 us (4%)
  matrix products  2.15 us (2%)
  local copies, waits for them, and re-layouts  1.83 us (1%)
    all_to_all x6, blocking collectives, swap(): return lax.all_to_all(value, axis, split_axis=0, concat_axis=0, tiled=True)  127 us

profile of v7, /device:TPU:1, one launch (start us, length us, event | category | flops | bytes accessed | tf_op | source)
XLA Modules:
  0.0 138.0 jit_solution(13817763381590473999)
XLA Ops:
  0.6 2.1 %shard_map.120 = bf16[16,136,128]{2,1,0:T(8,128)(2,1)} custom-call(s32[2,8]{1,0:T(2,128)} %bitcast.44, bf16[64,1024]{1,0:T(8,128)(2,1)} %q_ref.1, bf16[64,1024]{1,0:T(8,128)(2,1)} %g_ref.1, bf16[64,1024]{1,0:T(8,128)(2,1)} %k_ref.1, bf16[64,1024]{1,0:T(8,128)(2,1)} %v_ref.1), custom_call_target="tpu_custom_call" | custom-call | tf_op jit(solution)/shard_map/pallas_call | solution.py:209
  2.7 38.1 %all_to_all.30.own_ref = bf16[16,136,128]{2,1,0:T(8,128)(2,1)S(1)} all-to-all(bf16[16,136,128]{2,1,0:T(8,128)(2,1)} %shard_map.120), channel_id=1, replica_groups=mesh['x'=4,'yh'=4,'yl'=2,'core'=2,'zh'=4,'zl'=2] {'yh','zh'}, dimensions={0} | all-to-all | bytes 1114112 | tf_op jit(solution)/shard_map/all_to_all | solution.py:185
  40.8 0.2 copy.13
  41.1 0.0 copy-start
  41.1 15.6 %all_to_all.31 = bf16[32,40,128]{2,1,0:T(8,128)(2,1)S(1)} all-to-all(bf16[32,40,128]{2,1,0:T(8,128)(2,1)S(1)} %pad_maximum_fusion.1), channel_id=1, replica_groups=mesh['x'=4,'yh'=4,'yl'=2,'core'=2,'zh'=4,'zl'=2] {'zl','yl','x','core'}, dimensions={0} | all-to-all | bytes 655360 | tf_op jit(solution)/shard_map/all_to_all | solution.py:185
  56.7 0.1 fusion.25
  56.8 0.1 pad.7.clone
  56.9 0.1 pad_add_fusion
  57.0 0.1 eq.32
  57.1 0.8 fusion.6
  57.8 18.6 %all_to_all.32 = bf16[32,56,256]{2,1,0:T(8,128)(2,1)S(1)} all-to-all(bf16[32,56,256]{2,1,0:T(8,128)(2,1)S(1)} %bitcast.36), channel_id=1, replica_groups=mesh['x'=4,'yh'=4,'yl'=2,'core'=2,'zh'=4,'zl'=2] {'zl','yl','x','core'}, dimensions={0} | all-to-all | bytes 1835008 | tf_op jit(solution)/shard_map/all_to_all | solution.py:185
  76.5 0.2 reshape.64
  76.7 0.2 copy.14
  76.9 2.4 %shard_map.121 = (bf16[16,64,128]{2,1,0:T(8,128)(2,1)S(1)}, bf16[56,64,128]{2,1,0:T(8,128)(2,1)S(1)}, f32[16,64,128]{2,1,0:T(8,128)S(1)}) custom-call(bf16[16,136,128]{2,1,0:T(8,128)(2,1)S(1)} %all_to_all.30.own_ref, bf16[56,64,128]{2,1,0:T(8,128)(2,1)S(1)} %bitcast.29), custom_call_target="tpu_custom_call" | custom-call | tf_op jit(solution)/shard_map/pallas_call | solution.py:245
  79.4 0.6 copy.15
  80.0 18.7 %all_to_all.33 = bf16[32,112,128]{2,1,0:T(8,128)(2,1)S(1)} all-to-all(bf16[32,112,128]{2,1,0:T(8,128)(2,1)S(1)} %bitcast.32), channel_id=1, replica_groups=mesh['x'=4,'yh'=4,'yl'=2,'core'=2,'zh'=4,'zl'=2] {'zl','yl','x','core'}, dimensions={0} | all-to-all | bytes 1835008 | tf_op jit(solution)/shard_map/all_to_all | solution.py:185
  98.6 0.1 fusion.27
  98.7 0.7 fusion.15
  99.4 0.7 fusion.18
  100.1 11.6 %all_to_all.34 = bf16[32,32,128]{2,1,0:T(8,128)(2,1)S(1)} all-to-all(bf16[32,32,128]{2,1,0:T(8,128)(2,1)S(1)} %pad_maximum_fusion.2), channel_id=1, replica_groups=mesh['x'=4,'yh'=4,'yl'=2,'core'=2,'zh'=4,'zl'=2] {'zl','yl','x','core'}, dimensions={0} | all-to-all | bytes 524288 | tf_op jit(solution)/shard_map/all_to_all | solution.py:185
  111.8 0.3 copy.16
  112.1 0.1 fusion.21
  112.3 24.8 %all_to_all.35.in_ref = bf16[16,128,128]{2,1,0:T(8,128)(2,1)S(1)} all-to-all(bf16[16,128,128]{2,1,0:T(8,128)(2,1)S(1)} %pad_maximum_fusion), channel_id=1, replica_groups=mesh['x'=4,'yh'=4,'yl'=2,'core'=2,'zh'=4,'zl'=2] {'yh','zh'}, dimensions={0} | all-to-all | bytes 1048576 | tf_op jit(solution)/shard_map/all_to_all | solution.py:185
  137.1 0.9 shard_map.122
  (14 shorter events, 0.2 us)
Async XLA Ops:
  41.0 15.8 %copy-start.1 = (s32[2]{0:T(128)S(1)}, s32[2]{0:T(128)}, u32[]{:S(2)}) copy-start(s32[2]{0:T(128)} %param.14) | copy-start | bytes 28
  41.1 15.8 %copy-start = (s32[32,22]{1,0:T(8,128)S(1)}, s32[32,22]{1,0:T(8,128)}, u32[]{:S(2)}) copy-start(s32[32,22]{1,0:T(8,128)} %constant.11.clone) | copy-start | bytes 8452
  41.1 16.0 %copy-start.2 = (s32[512]{0:T(512)S(1)}, s32[512]{0:T(512)}, u32[]{:S(2)}) copy-start(s32[512]{0:T(512)} %constant.19) | copy-start | bytes 6148

commit v8 on v4

--- a/solution.py
+++ b/solution.py
@@ -268,7 +268,7 @@
     ]
     total = swap(jnp.concatenate(total, axis=1), plane)
     total = total.reshape(COLUMNS, ROWS, COLUMN, LANES).transpose(2, 1, 0, 3)
-    total = total.reshape(COLUMN, BLOCK, LANES).astype(jnp.float32)
+    total = lax.optimization_barrier(total.reshape(COLUMN, BLOCK, LANES)).astype(jnp.float32)
     pair_grad = (own_grad + total).astype(half)
     result = swap(jnp.concatenate([outs, pair_grad], axis=1), column)
     return vmem_call(unpack_kernel, (jax.ShapeDtypeStruct(query_rows.shape, half),) * 4)(result)

time: 138 us -> 138 us (level)
  no operation moved by 1% of the time
where the time goes in v8:
time: 138 us
  blocking collectives  127 us (92%)
  Pallas kernels  5.46 us (4%)
  matrix products  2.15 us (2%)
  local copies, waits for them, and re-layouts  1.63 us (1%)
    all_to_all x6, blocking collectives, swap(): return lax.all_to_all(value, axis, split_axis=0, concat_axis=0, tiled=True)  127 us

profile of v8, /device:TPU:1, one launch (start us, length us, event | category | flops | bytes accessed | tf_op | source)
XLA Modules:
  0.0 137.7 jit_solution(4621348601874990115)
XLA Ops:
  0.6 2.1 %shard_map.120 = bf16[16,136,128]{2,1,0:T(8,128)(2,1)} custom-call(s32[2,8]{1,0:T(2,128)} %bitcast.41, bf16[64,1024]{1,0:T(8,128)(2,1)} %q_ref.1, bf16[64,1024]{1,0:T(8,128)(2,1)} %g_ref.1, bf16[64,1024]{1,0:T(8,128)(2,1)} %k_ref.1, bf16[64,1024]{1,0:T(8,128)(2,1)} %v_ref.1), custom_call_target="tpu_custom_call" | custom-call | tf_op jit(solution)/shard_map/pallas_call | solution.py:209
  2.7 38.1 %all_to_all.30.own_ref = bf16[16,136,128]{2,1,0:T(8,128)(2,1)S(1)} all-to-all(bf16[16,136,128]{2,1,0:T(8,128)(2,1)} %shard_map.120), channel_id=1, replica_groups=mesh['x'=4,'yh'=4,'yl'=2,'core'=2,'zh'=4,'zl'=2] {'yh','zh'}, dimensions={0} | all-to-all | bytes 1114112 | tf_op jit(solution)/shard_map/all_to_all | solution.py:185
  40.8 0.2 copy.13
  41.1 0.0 copy-start
  41.1 15.5 %all_to_all.31 = bf16[32,40,128]{2,1,0:T(8,128)(2,1)S(1)} all-to-all(bf16[32,40,128]{2,1,0:T(8,128)(2,1)S(1)} %pad_maximum_fusion.1), channel_id=1, replica_groups=mesh['x'=4,'yh'=4,'yl'=2,'core'=2,'zh'=4,'zl'=2] {'x','yl','zl','core'}, dimensions={0} | all-to-all | bytes 655360 | tf_op jit(solution)/shard_map/all_to_all | solution.py:185
  56.6 0.1 fusion.24
  56.7 0.1 pad.7.clone
  56.8 0.1 pad_add_fusion
  56.9 0.1 eq.32
  57.0 0.8 fusion.6
  57.7 18.7 %all_to_all.32 = bf16[32,56,256]{2,1,0:T(8,128)(2,1)S(1)} all-to-all(bf16[32,56,256]{2,1,0:T(8,128)(2,1)S(1)} %bitcast.33), channel_id=1, replica_groups=mesh['x'=4,'yh'=4,'yl'=2,'core'=2,'zh'=4,'zl'=2] {'x','yl','zl','core'}, dimensions={0} | all-to-all | bytes 1835008 | tf_op jit(solution)/shard_map/all_to_all | solution.py:185
  76.4 0.2 reshape.64
  76.6 0.2 copy.14
  76.9 2.4 %shard_map.121 = (bf16[16,64,128]{2,1,0:T(8,128)(2,1)S(1)}, bf16[56,64,128]{2,1,0:T(8,128)(2,1)S(1)}, f32[16,64,128]{2,1,0:T(8,128)S(1)}) custom-call(bf16[16,136,128]{2,1,0:T(8,128)(2,1)S(1)} %all_to_all.30.own_ref, bf16[56,64,128]{2,1,0:T(8,128)(2,1)S(1)} %bitcast.25), custom_call_target="tpu_custom_call" | custom-call | tf_op jit(solution)/shard_map/pallas_call | solution.py:245
  79.3 0.6 copy.15
  79.9 18.9 %all_to_all.33 = bf16[32,112,128]{2,1,0:T(8,128)(2,1)S(1)} all-to-all(bf16[32,112,128]{2,1,0:T(8,128)(2,1)S(1)} %bitcast.28), channel_id=1, replica_groups=mesh['x'=4,'yh'=4,'yl'=2,'core'=2,'zh'=4,'zl'=2] {'x','yl','zl','core'}, dimensions={0} | all-to-all | bytes 1835008 | tf_op jit(solution)/shard_map/all_to_all | solution.py:185
  98.8 0.1 fusion.26
  98.9 0.7 fusion.15
  99.6 0.7 fusion.18
  100.3 11.8 %all_to_all.34 = bf16[32,32,128]{2,1,0:T(8,128)(2,1)S(1)} all-to-all(bf16[32,32,128]{2,1,0:T(8,128)(2,1)S(1)} %pad_maximum_fusion.2), channel_id=1, replica_groups=mesh['x'=4,'yh'=4,'yl'=2,'core'=2,'zh'=4,'zl'=2] {'x','yl','zl','core'}, dimensions={0} | all-to-all | bytes 524288 | tf_op jit(solution)/shard_map/all_to_all | solution.py:185
  112.1 0.1 copy.16
  112.3 0.1 add_convert_fusion
  112.4 24.4 %all_to_all.35.in_ref = bf16[16,128,128]{2,1,0:T(8,128)(2,1)S(1)} all-to-all(bf16[16,128,128]{2,1,0:T(8,128)(2,1)S(1)} %pad_maximum_fusion), channel_id=1, replica_groups=mesh['x'=4,'yh'=4,'yl'=2,'core'=2,'zh'=4,'zl'=2] {'yh','zh'}, dimensions={0} | all-to-all | bytes 1048576 | tf_op jit(solution)/shard_map/all_to_all | solution.py:185
  136.8 0.9 shard_map.122
  (13 shorter events, 0.2 us)
Async XLA Ops:
  41.0 15.7 %copy-start.1 = (s32[2]{0:T(128)S(1)}, s32[2]{0:T(128)}, u32[]{:S(2)}) copy-start(s32[2]{0:T(128)} %param.14) | copy-start | bytes 28
  41.1 15.7 %copy-start = (s32[32,22]{1,0:T(8,128)S(1)}, s32[32,22]{1,0:T(8,128)}, u32[]{:S(2)}) copy-start(s32[32,22]{1,0:T(8,128)} %constant.11.clone) | copy-start | bytes 8452
  41.1 15.9 %copy-start.2 = (s32[512]{0:T(512)S(1)}, s32[512]{0:T(512)}, u32[]{:S(2)}) copy-start(s32[512]{0:T(512)} %constant.19) | copy-start | bytes 6148
